TPU v7x, 128 devices: a whole 4x4x4 slice. The times are simulated.
128 devices in a mesh: grp: 32 (over z, x_hi, y), tp: 4 (over x_lo, core).
Axes of the slice: x: 4 (x_hi: 2, x_lo: 2; x = x_hi * 2 + x_lo), y: 4, z: 4, core: 2. Of those that a mesh axis runs over, the one named last changes fastest.
Arguments:
- states: bfloat16 [32768, 5120], P(('grp', 'tp')), may hold values from -27 to 27
- norm_gain: float32 [5120], replicated, may hold values from 0.5 to 1.5
- query_gain: float32 [128], replicated, may hold values from 0.1 to 1.9
- key_norm_gain: float32 [128], replicated, may hold values from 0.1 to 1.9
- lengths: int32 [1024], P('grp'), may hold values from 8 to 32
- w_query: bfloat16 [5120, 4096], P('grp', 'tp'), may hold values from -0.078125 to 0.078125
- key_weight: bfloat16 [5120, 512], P('grp', 'tp'), may hold values from -0.078125 to 0.078125
- value_weight: bfloat16 [5120, 512], P('grp', 'tp'), may hold values from -0.078125 to 0.078125
- w_out: bfloat16 [5120, 4096], P('grp', 'tp'), may hold values from -0.09375 to 0.09375
Outputs:
- attention_out: bfloat16 [32768, 5120], P(('grp', 'tp'))
All inputs are finite; a program needn't handle non-finite values.
Results may differ from a plain program's by a relative error of at most 0.014.
Values may be sent and summed in bfloat16 or wider, within the bound.
No kernel may reach another device: no remote copies, remote signals or barrier semaphores. Data moves between devices by JAX's collectives and lax.ppermute only.
A program may use at most 128 MiB of HBM per device.

v0:
```python
import functools
import math

import jax
import jax.numpy as jnp
from jax import lax
from jax.experimental import pallas as pl
from jax.experimental.pallas import tpu as pltpu
from jax.sharding import Mesh, PartitionSpec as P

AXES = ("z", "xh", "y", "xl", "c")
SIZES = (4, 2, 4, 2, 2)
X = ("xh", "xl")


def shift(value, axis, steps, size=4):
    return lax.ppermute(value, axis, [(i, (i + steps) % size) for i in range(size)])


def norm_kernel(place, x_ref, gain_ref, o_ref):
    z, y = place[0], place[1]
    x = x_ref[...].astype(jnp.float32)
    scale = lax.rsqrt(jnp.mean(x * x, axis=-1, keepdims=True) + 1e-06)
    width = x.shape[1] // 8
    piece = width // 4
    for block in range(8):
        part = x[:, block * width : (block + 1) * width]
        part = part * scale * gain_ref[:, block * width : (block + 1) * width]
        part = pltpu.roll(part, lax.rem(4 - y, 4) * piece, 1)
        target = lax.rem(block // 2 - z + 4, 4) * 2 + block % 2
        o_ref[:, pl.ds(pl.multiple_of(target * width, 128), width)] = part.astype(jnp.bfloat16)


def rolled_norm(states, gain, z, y):
    rows, width = states.shape
    step = 64
    return pl.pallas_call(
        norm_kernel,
        out_shape=jax.ShapeDtypeStruct((rows, width), jnp.bfloat16),
        grid_spec=pltpu.PrefetchScalarGridSpec(
            num_scalar_prefetch=1,
            grid=(rows // step,),
            in_specs=[
                pl.BlockSpec((step, width), lambda i, p: (i, 0)),
                pl.BlockSpec((1, width), lambda i, p: (0, 0)),
            ],
            out_specs=pl.BlockSpec((step, width), lambda i, p: (i, 0)),
        ),
        compiler_params=pltpu.CompilerParams(vmem_limit_bytes=32 * 1024 * 1024),
        cost_estimate=pl.CostEstimate(flops=rows * width * 6, bytes_accessed=rows * width * 4, transcendentals=rows),
        name="norm",
    )(jnp.stack([z, y]).astype(jnp.int32), states, gain.reshape(1, width))


def attend_kernel(splits, live_ref, qgain_ref, kgain_ref, cos_ref, sin_ref, *refs):
    parts, o_ref = refs[:-1], refs[-1]
    heads = []
    for ref, count in zip(parts, splits):
        heads += [ref[:, i * 128 : (i + 1) * 128] for i in range(count)]
    rows = o_ref.shape[0]
    cosine, sine = cos_ref[...], sin_ref[...]

    def prepare(v, gain):
        v = v * lax.rsqrt(jnp.mean(v * v, axis=-1, keepdims=True) + 1e-06) * gain
        return (v * cosine + pltpu.roll(v, 64, 1) * sine).astype(jnp.bfloat16)

    count = len(heads) - 2
    queries = jnp.concatenate([prepare(h, qgain_ref[...]) for h in heads[:count]], axis=0)
    keys = prepare(heads[count], kgain_ref[...])
    values = heads[count + 1].astype(jnp.bfloat16)
    scores = lax.dot_general(
        queries, keys, (((1,), (1,)), ((), ())), preferred_element_type=jnp.float32
    ) * (1.0 / math.sqrt(128.0))
    i = lax.broadcasted_iota(jnp.int32, (rows, rows), 0)
    j = lax.broadcasted_iota(jnp.int32, (rows, rows), 1)
    allowed = (j <= i) & (j >= (i & ~31)) & (live_ref[0] > 0)
    outs = []
    for h in range(count):
        weights = jnp.where(allowed, jnp.exp(scores[h * rows : (h + 1) * rows]), 0.0)
        outs.append((weights / jnp.sum(weights, axis=-1, keepdims=True)).astype(jnp.bfloat16))
    attended = jnp.dot(jnp.concatenate(outs, axis=0), values, preferred_element_type=jnp.float32)
    for h in range(count):
        o_ref[:, h * 128 : (h + 1) * 128] = attended[h * rows : (h + 1) * rows].astype(jnp.bfloat16)


def attend(parts, row_lengths, query_gain, key_norm_gain):
    total, head_width = parts[0].shape[0], query_gain.shape[0]
    slots, step = 32, 128
    splits = [p.shape[1] // head_width for p in parts]
    count = sum(splits) - 2
    half_width = head_width // 2
    freq_index = jnp.arange(half_width, dtype=jnp.float32)
    frequency = jnp.exp(freq_index * (-2.0 * math.log(1000000.0) / head_width))
    angles = jnp.arange(slots, dtype=jnp.float32)[:, None] * frequency[None, :]
    cosine, sine = jnp.cos(angles), jnp.sin(angles)
    cosine = jnp.tile(jnp.concatenate([cosine, cosine], axis=1), (step // slots, 1))
    sine = jnp.tile(jnp.concatenate([-sine, sine], axis=1), (step // slots, 1))
    live = (jnp.arange(slots, dtype=jnp.int32)[None, :] < row_lengths[:, None]).astype(jnp.int32)
    live = live.reshape(total // step, 1, step)
    whole = lambda shape: pl.BlockSpec(shape, lambda i: (0,) * len(shape))
    return pl.pallas_call(
        functools.partial(attend_kernel, splits),
        out_shape=jax.ShapeDtypeStruct((total, count * head_width), jnp.bfloat16),
        grid=(total // step,),
        in_specs=[
            pl.BlockSpec((1, 1, step), lambda i: (i, 0, 0)),
            whole((1, head_width)),
            whole((1, head_width)),
            whole((step, head_width)),
            whole((step, head_width)),
        ]
        + [pl.BlockSpec((step, p.shape[1]), lambda i: (i, 0)) for p in parts],
        out_specs=pl.BlockSpec((step, count * head_width), lambda i: (i, 0)),
        compiler_params=pltpu.CompilerParams(vmem_limit_bytes=40 * 1024 * 1024),
        cost_estimate=pl.CostEstimate(
            flops=4 * total * step * count * head_width,
            bytes_accessed=total * count * head_width * 8,
            transcendentals=total * step * count,
        ),
        name="attend",
    )(live, query_gain.reshape(1, -1), key_norm_gain.reshape(1, -1), cosine, sine, *parts)


def first_hop(block, axis):
    return [block, shift(block, axis, -1), shift(block, axis, 2), shift(block, axis, 1)]


def second_hop(block, axis):
    after, before = shift(block, axis, -1), shift(block, axis, 1)
    half = block.shape[0] // 2
    far = [shift(after[:half], axis, -1), shift(before[half:], axis, 1)]
    return [block, after, jnp.concatenate(far, axis=0), before]


def per_device(
    states, norm_gain, query_gain, key_norm_gain, lengths, w_query, key_weight, value_weight, w_out
):
    z, y, xh, xl, c = (lax.axis_index(a) for a in ("z", "y", "xh", "xl", "c"))
    rows, width = states.shape
    piece = w_query.shape[0]
    half_rows = rows // 2

    out_full = lax.all_gather(w_out, ("z", "xh", "y"), axis=0, tiled=True)

    w_local = jnp.concatenate([w_query, key_weight, value_weight], axis=1)
    w_other = shift(w_local, "xh", 1, 2)
    w_pair = lax.dynamic_slice_in_dim(
        jnp.concatenate([w_local, w_other, w_local], axis=0), xh * piece, 2 * piece, axis=0
    )
    half = w_local.shape[1] // 2
    first, second = w_pair[:, :half], w_pair[:, half:]

    normed = rolled_norm(states, norm_gain, z, y)
    from_left = shift(normed[half_rows:], X, 1)
    from_right = shift(normed[:half_rows], X, -1)
    other_lengths = shift(lengths, "xh", 1, 2)
    mine = jnp.concatenate([normed, from_left, from_right], axis=0)
    all_rows = jnp.concatenate([mine, shift(mine, "c", 1, 2)], axis=0)

    along_y = first_hop(first, "y")
    first_block = jnp.concatenate([b[:piece] for b in along_y] + [b[piece:] for b in along_y], axis=0)
    second_block = jnp.concatenate(first_hop(second, "z"), axis=0)
    first_parts = second_hop(first_block, "z")
    second_parts = second_hop(second_block, "y")
    depth = first_block.shape[0]
    first_result = sum(
        jnp.dot(all_rows[:, i * depth : (i + 1) * depth], part, preferred_element_type=jnp.float32)
        for i, part in enumerate(first_parts)
    )
    second_weights = jnp.stack(
        [p.reshape(8, piece, half) for p in second_parts], axis=1
    ).reshape(width, half)
    second_result = jnp.dot(all_rows, second_weights, preferred_element_type=jnp.float32)

    total = all_rows.shape[0]
    slots = 32
    per = rows // slots
    hp = per // 2

    def prompt_lengths(core):
        own = lax.dynamic_slice_in_dim(lengths, (xl * 2 + core) * per, per)
        near = lax.dynamic_slice_in_dim(lengths, ((1 - xl) * 2 + core) * per, per)
        away = lax.dynamic_slice_in_dim(other_lengths, ((1 - xl) * 2 + core) * per, per)
        left = jnp.where(xl == 1, near, away)[hp:]
        right = jnp.where(xl == 0, near, away)[:hp]
        return [own, left, right]

    row_lengths = jnp.concatenate(prompt_lengths(c) + prompt_lengths(1 - c))

    attended = attend([first_result, second_result], row_lengths, query_gain, key_norm_gain)

    contract = (((1,), (1,)), ((), ()))
    chunks = 4
    size = width // chunks
    outs = []
    for i in range(chunks):
        partial = lax.dot_general(
            attended, out_full[i * size : (i + 1) * size], contract, preferred_element_type=jnp.float32
        ).astype(jnp.bfloat16)
        received = shift(partial[total // 2 :], "c", 1, 2)
        chip = partial[: total // 2].astype(jnp.float32) + received.astype(jnp.float32)
        back = chip[rows:].astype(jnp.bfloat16)
        right = shift(back[:half_rows], X, -1)
        left = shift(back[half_rows:], X, 1)
        outs.append(
            (chip[:rows] + jnp.concatenate([left, right], axis=0).astype(jnp.float32)).astype(jnp.bfloat16)
        )
    return jnp.concatenate(outs, axis=1)


def solution(mesh):
    fine = Mesh(mesh.devices.reshape(SIZES), AXES)
    grp, tp = ("z", "xh", "y"), ("xl", "c")
    placed = (
        P(grp + tp, None),
        P(),
        P(),
        P(),
        P(grp),
        P(grp, tp),
        P(grp, tp),
        P(grp, tp),
        P(grp, tp),
    )
    return jax.shard_map(
        per_device, mesh=fine, in_specs=placed, out_specs=P(grp + tp, None), check_vma=False
    )
```

profile of v0, /device:TPU:1, one launch (start us, length us, event | category | flops | bytes accessed | tf_op | source)
XLA Modules:
  0.0 302.8 jit_solution(4347207073186828817)
XLA Ops:
  7.3 1.7 copy-done
  9.8 2.8 norm.1
  12.7 1.7 fusion.29
  14.4 3.3 %collective-permute-start.2 = (bf16[128,5120]{1,0:T(8,128)(2,1)}, bf16[128,5120]{1,0:T(8,128)(2,1)}, u32[]{:S(2)}, u32[]{:S(2)}) collective-permute-start(bf16[128,5120]{1,0:T(8,128)(2,1)} %get-tuple-element.14), channel_id=1, source_target_pairs={{0,18},{2,0},{16,2},{18,16},{1,19},{3,1},{17,3},{19,17},{4,22},{6,... | collective-permute-start | bytes 3932168 | tf_op jit(solution)/shard_map/ppermute | solution.py:17
  17.8 1.8 collective-permute-start.4
  19.6 45.6 %collective-permute-done.4 = bf16[160,1280]{1,0:T(8,128)(2,1)S(1)} collective-permute-done((bf16[160,1280]{1,0:T(8,128)(2,1)S(1)}, bf16[160,1280]{1,0:T(8,128)(2,1)S(1)}, u32[]{:S(2)}, u32[]{:S(2)}) %collective-permute-start.4) | collective-permute-done | bytes 409632 | tf_op jit(solution)/shard_map/ppermute | solution.py:17
  66.3 2.1 collective-permute-start.14
  68.4 4.0 %collective-permute-start.13 = (bf16[320,640]{1,0:T(8,128)(2,1)S(1)}, bf16[320,640]{1,0:T(8,128)(2,1)S(1)}, u32[]{:S(2)}, u32[]{:S(2)}) collective-permute-start(bf16[320,640]{1,0:T(8,128)(2,1)S(1)} %get-tuple-element.23), channel_id=1, source_target_pairs={{0,64},{32,96},{64,0},{96,32},{1,65},{33,97},{65,1},{97,33},{2,66}... | collective-permute-start | bytes 1228808 | tf_op jit(solution)/shard_map/ppermute | solution.py:17
  72.8 4.4 %pad_maximum_fusion.2 = bf16[512,5120]{1,0:T(8,128)(2,1)} fusion(bf16[128,5120]{1,0:T(8,128)(2,1)} %collective-permute-done.2, bf16[128,5120]{1,0:T(8,128)(2,1)} %collective-permute-done.1, bf16[256,5120]{1,0:T(8,128)(2,1)S(1)} %norm.1), kind=kLoop, calls=%fused_computation.2 | loop fusion | flops 15728640 | bytes 10485760 | tf_op jit(solution)/shard_map/concatenate | solution.py:157
  77.2 4.7 %collective-permute-start.3 = (bf16[512,5120]{1,0:T(8,128)(2,1)}, bf16[512,5120]{1,0:T(8,128)(2,1)}, u32[]{:S(2)}, u32[]{:S(2)}) collective-permute-start(bf16[512,5120]{1,0:T(8,128)(2,1)} %pad_maximum_fusion.2), channel_id=1, source_target_pairs={{0,1},{1,0},{2,3},{3,2},{4,5},{5,4},{6,7},{7,6},{8,9},{9,8},{10,11... | collective-permute-start | bytes 15728648 | tf_op jit(solution)/shard_map/ppermute | solution.py:17
  81.9 2.7 collective-permute-start.5
  85.3 1.6 collective-permute-start.6
  86.9 7.3 %collective-permute-done.13 = bf16[320,640]{1,0:T(8,128)(2,1)S(1)} collective-permute-done((bf16[320,640]{1,0:T(8,128)(2,1)S(1)}, bf16[320,640]{1,0:T(8,128)(2,1)S(1)}, u32[]{:S(2)}, u32[]{:S(2)}) %collective-permute-start.13) | collective-permute-done | bytes 409632 | tf_op jit(solution)/shard_map/ppermute | solution.py:17
  94.2 1.5 collective-permute-start.7
  95.9 1.5 collective-permute-start.17
  97.5 2.4 collective-permute-done.5
  99.9 4.7 %collective-permute-start.15 = (bf16[1280,640]{1,0:T(8,128)(2,1)S(1)}, bf16[1280,640]{1,0:T(8,128)(2,1)S(1)}, u32[]{:S(2)}, u32[]{:S(2)}) collective-permute-start(bf16[1280,640]{1,0:T(8,128)(2,1)S(1)} %pad_maximum_fusion.4), channel_id=1, source_target_pairs={{0,12},{4,0},{8,4},{12,8},{1,13},{5,1},{9,5},{13,9},{2,14},{6,2},{... | collective-permute-start | bytes 4915208 | tf_op jit(solution)/shard_map/ppermute | solution.py:17
  106.0 9.2 %collective-permute-done.7 = bf16[320,640]{1,0:T(8,128)(2,1)S(1)} collective-permute-done((bf16[320,640]{1,0:T(8,128)(2,1)S(1)}, bf16[320,640]{1,0:T(8,128)(2,1)S(1)}, u32[]{:S(2)}, u32[]{:S(2)}) %collective-permute-start.7) | collective-permute-done | bytes 409632 | tf_op jit(solution)/shard_map/ppermute | solution.py:17
  118.6 2.7 collective-permute-start.8
  121.3 48.7 %collective-permute-done.17 = bf16[1280,640]{1,0:T(8,128)(2,1)S(1)} collective-permute-done((bf16[1280,640]{1,0:T(8,128)(2,1)S(1)}, bf16[1280,640]{1,0:T(8,128)(2,1)S(1)}, u32[]{:S(2)}, u32[]{:S(2)}) %collective-permute-start.17) | collective-permute-done | bytes 1638432 | tf_op jit(solution)/shard_map/ppermute | solution.py:17
  170.0 1.8 collective-permute-start
  174.7 1.7 collective-permute-start.16
  178.7 1.4 slice.224
  180.0 2.6 collective-permute-start.9
  182.6 9.7 %collective-permute-done.18 = bf16[640,640]{1,0:T(8,128)(2,1)S(1)} collective-permute-done((bf16[640,640]{1,0:T(8,128)(2,1)}, bf16[640,640]{1,0:T(8,128)(2,1)S(1)}, u32[]{:S(2)}, u32[]{:S(2)}) %collective-permute-start.18) | collective-permute-done | bytes 819232 | tf_op jit(solution)/shard_map/ppermute | solution.py:17
  192.3 1.9 collective-permute-done.16
  196.6 5.0 %pad_maximum_fusion = bf16[1024,5120]{1,0:T(8,128)(2,1)S(1)} fusion(bf16[512,5120]{1,0:T(8,128)(2,1)} %collective-permute-done.3, bf16[128,5120]{1,0:T(8,128)(2,1)} %collective-permute-done.2, bf16[128,5120]{1,0:T(8,128)(2,1)} %collective-permute-done.1, bf16[256,5120]{1,0:T(8,128)(2,1)S(1)} %norm.1), kind=kLoop, calls=%fused_computation | loop fusion | flops 41943040 | bytes 20971520 | tf_op jit(solution)/shard_map/concatenate | solution.py:158
  201.7 2.2 fusion.6
  203.9 3.6 %fusion.10 = f32[1024,640]{1,0:T(8,128)S(1)} fusion(bf16[1280,640]{1,0:T(8,128)(2,1)} %slice_dynamic-update-slice_fusion, bf16[1024,5120]{1,0:T(8,128)(2,1)S(1)} %pad_maximum_fusion), kind=kOutput, calls=%fused_computation.17 | convolution fusion | flops 1677721600 | bytes 6881280 | tf_op jit(solution)/shard_map/dot_general | solution.py:167
  207.6 3.6 %fusion.8 = f32[1024,640]{1,0:T(8,128)S(1)} fusion(bf16[1280,640]{1,0:T(8,128)(2,1)} %collective-permute-done.8, bf16[1024,5120]{1,0:T(8,128)(2,1)S(1)} %pad_maximum_fusion), kind=kOutput, calls=%fused_computation.15 | convolution fusion | flops 1677721600 | bytes 6881280 | tf_op jit(solution)/shard_map/dot_general | solution.py:167
  211.2 3.8 %add_add_fusion.refs_0_ = f32[1024,640]{1,0:T(8,128)S(1)} fusion(f32[1024,640]{1,0:T(8,128)S(1)} %fusion.6, f32[1024,640]{1,0:T(8,128)S(1)} %fusion.10, f32[1024,640]{1,0:T(8,128)S(1)} %fusion.8, bf16[1280,640]{1,0:T(8,128)(2,1)} %collective-permute-done.10, bf16[1024,5120]{1,0:T(8,128)(2,1)S(1)} %pad_maximum_fusion), kind=kOutput, calls=%fused_computation.24 | convolution fusion | flops 1679687680 | bytes 14745600 | tf_op jit(solution)/shard_map/dot_general | solution.py:167
  215.0 18.0 %fusion.35.refs_1_ = f32[1024,640]{1,0:T(8,128)S(1)} fusion(bf16[1024,5120]{1,0:T(8,128)(2,1)S(1)} %pad_maximum_fusion, bf16[5120,640]{1,0:T(8,128)(2,1)S(1)} %bitcast.30), kind=kOutput, calls=%fused_computation.78 | convolution fusion | flops 6710886400 | bytes 19660800 | tf_op jit(solution)/shard_map/dot_general | solution.py:173
  233.1 10.9 %attend.1 = bf16[1024,1024]{1,0:T(8,128)(2,1)S(1)} custom-call(s32[8,1,128]{2,1,0:T(1,128)S(1)} %compare_convert_fusion.live_ref, f32[1,128]{1,0:T(1,128)S(1)} %bitcast.26, f32[1,128]{1,0:T(1,128)S(1)} %bitcast.27, f32[128,128]{1,0:T(8,128)S(1)} %bitcast.23, f32[128,128]{1,0:T(8,128)S(1)} %bitcast.24, f32[1024,640]{1,0:T(8,128)S(1)} %add_add_fusion.refs_0_, ...), custom_call_target="tpu_custom_call" | custom-call | flops 536870912 | bytes 8388608 | tf_op jit(solution)/shard_map/attend/pallas_call | solution.py:101
  244.1 5.1 %convolution_convert_fusion = bf16[1024,1280]{1,0:T(8,128)(2,1)S(1)} fusion(bf16[1024,1024]{1,0:T(8,128)(2,1)S(1)} %attend.1, bf16[5120,1024]{1,0:T(8,128)(2,1)} %all-gather.2.cloned.1.call-done), kind=kOutput, calls=%fused_computation.3 | convolution fusion | flops 2685665280 | bytes 7340032 | tf_op jit(solution)/shard_map/dot_general | solution.py:197
  249.3 2.5 collective-permute-start.28
  251.7 3.2 %convolution_convert_fusion.1 = bf16[1024,1280]{1,0:T(8,128)(2,1)S(1)} fusion(bf16[1024,1024]{1,0:T(8,128)(2,1)S(1)} %attend.1, bf16[5120,1024]{1,0:T(8,128)(2,1)S(1)} %copy-done.14), kind=kOutput, calls=%fused_computation.4 | convolution fusion | flops 2685665280 | bytes 7340032 | tf_op jit(solution)/shard_map/dot_general | solution.py:197
  255.1 3.2 %convolution_convert_fusion.2 = bf16[1024,1280]{1,0:T(8,128)(2,1)S(1)} fusion(bf16[1024,1024]{1,0:T(8,128)(2,1)S(1)} %attend.1, bf16[5120,1024]{1,0:T(8,128)(2,1)S(1)} %copy-done.14), kind=kOutput, calls=%fused_computation.5 | convolution fusion | flops 2685665280 | bytes 7340032 | tf_op jit(solution)/shard_map/dot_general | solution.py:197
  259.0 3.2 %convolution_convert_fusion.3 = bf16[1024,1280]{1,0:T(8,128)(2,1)S(1)} fusion(bf16[1024,1024]{1,0:T(8,128)(2,1)S(1)} %attend.1, bf16[5120,1024]{1,0:T(8,128)(2,1)S(1)} %copy-done.14), kind=kOutput, calls=%fused_computation.6 | convolution fusion | flops 2685665280 | bytes 7340032 | tf_op jit(solution)/shard_map/dot_general | solution.py:197
  262.8 1.5 collective-permute-start.29
  264.7 1.4 collective-permute-start.27
  266.6 2.6 collective-permute-start.24
  269.5 2.1 collective-permute-done.30
  272.9 1.4 collective-permute-start.21
  274.4 4.2 %collective-permute-done.27 = bf16[128,1280]{1,0:T(8,128)(2,1)S(1)} collective-permute-done((bf16[128,1280]{1,0:T(8,128)(2,1)S(1)}, bf16[128,1280]{1,0:T(8,128)(2,1)S(1)}, u32[]{:S(2)}, u32[]{:S(2)}) %collective-permute-start.27) | collective-permute-done | bytes 327712 | tf_op jit(solution)/shard_map/ppermute | solution.py:17
  280.1 5.6 %collective-permute-done.24 = bf16[128,1280]{1,0:T(8,128)(2,1)S(1)} collective-permute-done((bf16[128,1280]{1,0:T(8,128)(2,1)S(1)}, bf16[128,1280]{1,0:T(8,128)(2,1)S(1)}, u32[]{:S(2)}, u32[]{:S(2)}) %collective-permute-start.24) | collective-permute-done | bytes 327712 | tf_op jit(solution)/shard_map/ppermute | solution.py:17
  285.7 1.3 collective-permute-done.23
  287.1 5.6 %collective-permute-done.21 = bf16[128,1280]{1,0:T(8,128)(2,1)S(1)} collective-permute-done((bf16[128,1280]{1,0:T(8,128)(2,1)S(1)}, bf16[128,1280]{1,0:T(8,128)(2,1)S(1)}, u32[]{:S(2)}, u32[]{:S(2)}) %collective-permute-start.21) | collective-permute-done | bytes 327712 | tf_op jit(solution)/shard_map/ppermute | solution.py:17
  294.1 1.6 pad_maximum_fusion.3
  (114 shorter events, 23.5 us)
Async XLA Ops:
  6.5 237.5 %all-gather.2.cloned.1.call-start = ((), (), s32[]{:S(2)}) async-start(), calls=%async_computation | async-start | bytes 10813440 | tf_op jit(solution)/shard_map/all_gather | solution.py:143
  7.3 1.7 copy-start
  9.1 0.7 copy-start.1
  12.7 5.0 %copy-start.10 = (bf16[160,1024]{1,0:T(8,128)(2,1)S(1)}, bf16[160,1024]{1,0:T(8,128)(2,1)}, u32[]{:S(2)}) copy-start(bf16[160,1024]{1,0:T(8,128)(2,1)} %param.14) | copy-start | bytes 983044
  12.7 5.1 %copy-start.11 = (bf16[160,128]{1,0:T(8,128)(2,1)S(1)}, bf16[160,128]{1,0:T(8,128)(2,1)}, u32[]{:S(2)}) copy-start(bf16[160,128]{1,0:T(8,128)(2,1)} %param.15) | copy-start | bytes 122884
  12.7 5.1 %copy-start.12 = (bf16[160,128]{1,0:T(8,128)(2,1)S(1)}, bf16[160,128]{1,0:T(8,128)(2,1)}, u32[]{:S(2)}) copy-start(bf16[160,128]{1,0:T(8,128)(2,1)} %param.16) | copy-start | bytes 122884
  14.4 58.4 %collective-permute-start.2 = (bf16[128,5120]{1,0:T(8,128)(2,1)}, bf16[128,5120]{1,0:T(8,128)(2,1)}, u32[]{:S(2)}, u32[]{:S(2)}) collective-permute-start(bf16[128,5120]{1,0:T(8,128)(2,1)} %get-tuple-element.14), channel_id=1, source_target_pairs={{0,18},{2,0},{16,2},{18,16},{1,19},{3,1},{17,3},{19,17},{4,22},{6,... | collective-permute-start | bytes 3932168 | tf_op jit(solution)/shard_map/ppermute | solution.py:17
  17.7 55.1 %collective-permute-start.1 = (bf16[128,5120]{1,0:T(8,128)(2,1)}, bf16[128,5120]{1,0:T(8,128)(2,1)}, u32[]{:S(2)}, u32[]{:S(2)}) collective-permute-start(bf16[128,5120]{1,0:T(8,128)(2,1)} %get-tuple-element.13), channel_id=1, source_target_pairs={{0,2},{2,16},{16,18},{18,0},{1,3},{3,17},{17,19},{19,1},{4,6},{6,2... | collective-permute-start | bytes 3932168 | tf_op jit(solution)/shard_map/ppermute | solution.py:17
  17.8 47.4 %collective-permute-start.4 = (bf16[160,1280]{1,0:T(8,128)(2,1)S(1)}, bf16[160,1280]{1,0:T(8,128)(2,1)S(1)}, u32[]{:S(2)}, u32[]{:S(2)}) collective-permute-start(bf16[160,1280]{1,0:T(8,128)(2,1)S(1)} %constant_dynamic-update-slice_fusion), channel_id=1, source_target_pairs={{0,16},{16,0},{1,17},{17,1},{2,18},{18,2},{3,19},{19,3},{4,20},{20... | collective-permute-start | bytes 1228808 | tf_op jit(solution)/shard_map/ppermute | solution.py:17
  66.3 19.0 %collective-permute-start.14 = (bf16[320,640]{1,0:T(8,128)(2,1)S(1)}, bf16[320,640]{1,0:T(8,128)(2,1)S(1)}, u32[]{:S(2)}, u32[]{:S(2)}) collective-permute-start(bf16[320,640]{1,0:T(8,128)(2,1)S(1)} %get-tuple-element.23), channel_id=1, source_target_pairs={{0,32},{32,64},{64,96},{96,0},{1,33},{33,65},{65,97},{97,1},{2,34}... | collective-permute-start | bytes 1228808 | tf_op jit(solution)/shard_map/ppermute | solution.py:17
  68.4 25.8 %collective-permute-start.13 = (bf16[320,640]{1,0:T(8,128)(2,1)S(1)}, bf16[320,640]{1,0:T(8,128)(2,1)S(1)}, u32[]{:S(2)}, u32[]{:S(2)}) collective-permute-start(bf16[320,640]{1,0:T(8,128)(2,1)S(1)} %get-tuple-element.23), channel_id=1, source_target_pairs={{0,64},{32,96},{64,0},{96,32},{1,65},{33,97},{65,1},{97,33},{2,66}... | collective-permute-start | bytes 1228808 | tf_op jit(solution)/shard_map/ppermute | solution.py:17
  72.4 23.3 %collective-permute-start.12 = (bf16[320,640]{1,0:T(8,128)(2,1)S(1)}, bf16[320,640]{1,0:T(8,128)(2,1)S(1)}, u32[]{:S(2)}, u32[]{:S(2)}) collective-permute-start(bf16[320,640]{1,0:T(8,128)(2,1)S(1)} %get-tuple-element.23), channel_id=1, source_target_pairs={{0,96},{32,0},{64,32},{96,64},{1,97},{33,1},{65,33},{97,65},{2,98}... | collective-permute-start | bytes 1228808 | tf_op jit(solution)/shard_map/ppermute | solution.py:17
  77.2 119.4 %collective-permute-start.3 = (bf16[512,5120]{1,0:T(8,128)(2,1)}, bf16[512,5120]{1,0:T(8,128)(2,1)}, u32[]{:S(2)}, u32[]{:S(2)}) collective-permute-start(bf16[512,5120]{1,0:T(8,128)(2,1)} %pad_maximum_fusion.2), channel_id=1, source_target_pairs={{0,1},{1,0},{2,3},{3,2},{4,5},{5,4},{6,7},{7,6},{8,9},{9,8},{10,11... | collective-permute-start | bytes 15728648 | tf_op jit(solution)/shard_map/ppermute | solution.py:17
  81.9 18.0 %collective-permute-start.5 = (bf16[320,640]{1,0:T(8,128)(2,1)S(1)}, bf16[320,640]{1,0:T(8,128)(2,1)S(1)}, u32[]{:S(2)}, u32[]{:S(2)}) collective-permute-start(bf16[320,640]{1,0:T(8,128)(2,1)S(1)} %get-tuple-element.24), channel_id=1, source_target_pairs={{0,12},{4,0},{8,4},{12,8},{1,13},{5,1},{9,5},{13,9},{2,14},{6,2},{... | collective-permute-start | bytes 1228808 | tf_op jit(solution)/shard_map/ppermute | solution.py:17
  85.3 84.6 %copy-start.13 = (s32[32]{0:T(128)S(1)}, s32[32]{0:T(128)}, u32[]{:S(2)}) copy-start(s32[32]{0:T(128)} %param.13) | copy-start | bytes 388
  85.3 19.9 %collective-permute-start.6 = (bf16[320,640]{1,0:T(8,128)(2,1)S(1)}, bf16[320,640]{1,0:T(8,128)(2,1)S(1)}, u32[]{:S(2)}, u32[]{:S(2)}) collective-permute-start(bf16[320,640]{1,0:T(8,128)(2,1)S(1)} %get-tuple-element.24), channel_id=1, source_target_pairs={{0,8},{4,12},{8,0},{12,4},{1,9},{5,13},{9,1},{13,5},{2,10},{6,14},... | collective-permute-start | bytes 1228808 | tf_op jit(solution)/shard_map/ppermute | solution.py:17
  94.2 20.9 %collective-permute-start.7 = (bf16[320,640]{1,0:T(8,128)(2,1)S(1)}, bf16[320,640]{1,0:T(8,128)(2,1)S(1)}, u32[]{:S(2)}, u32[]{:S(2)}) collective-permute-start(bf16[320,640]{1,0:T(8,128)(2,1)S(1)} %get-tuple-element.24), channel_id=1, source_target_pairs={{0,4},{4,8},{8,12},{12,0},{1,5},{5,9},{9,13},{13,1},{2,6},{6,10},{... | collective-permute-start | bytes 1228808 | tf_op jit(solution)/shard_map/ppermute | solution.py:17
  95.9 78.8 %copy-start.4 = (bf16[1280,640]{1,0:T(8,128)(2,1)}, bf16[1280,640]{1,0:T(8,128)(2,1)S(1)}, u32[]{:S(2)}) copy-start(bf16[1280,640]{1,0:T(8,128)(2,1)S(1)} %pad_maximum_fusion.4) | copy-start | bytes 4915204
  95.9 74.0 %collective-permute-start.17 = (bf16[1280,640]{1,0:T(8,128)(2,1)S(1)}, bf16[1280,640]{1,0:T(8,128)(2,1)S(1)}, u32[]{:S(2)}, u32[]{:S(2)}) collective-permute-start(bf16[1280,640]{1,0:T(8,128)(2,1)S(1)} %pad_maximum_fusion.4), channel_id=1, source_target_pairs={{0,4},{4,8},{8,12},{12,0},{1,5},{5,9},{9,13},{13,1},{2,6},{6,10},{... | collective-permute-start | bytes 4915208 | tf_op jit(solution)/shard_map/ppermute | solution.py:17
  99.9 72.9 %collective-permute-start.15 = (bf16[1280,640]{1,0:T(8,128)(2,1)S(1)}, bf16[1280,640]{1,0:T(8,128)(2,1)S(1)}, u32[]{:S(2)}, u32[]{:S(2)}) collective-permute-start(bf16[1280,640]{1,0:T(8,128)(2,1)S(1)} %pad_maximum_fusion.4), channel_id=1, source_target_pairs={{0,12},{4,0},{8,4},{12,8},{1,13},{5,1},{9,5},{13,9},{2,14},{6,2},{... | collective-permute-start | bytes 4915208 | tf_op jit(solution)/shard_map/ppermute | solution.py:17
  118.6 58.7 %collective-permute-start.10 = (bf16[1280,640]{1,0:T(8,128)(2,1)}, bf16[1280,640]{1,0:T(8,128)(2,1)}, u32[]{:S(2)}, u32[]{:S(2)}) collective-permute-start(bf16[1280,640]{1,0:T(8,128)(2,1)} %slice_dynamic-update-slice_fusion), channel_id=1, source_target_pairs={{0,32},{32,64},{64,96},{96,0},{1,33},{33,65},{65,97},{97,1},{2,34}... | collective-permute-start | bytes 4915208 | tf_op jit(solution)/shard_map/ppermute | solution.py:17
  118.6 60.0 %collective-permute-start.8 = (bf16[1280,640]{1,0:T(8,128)(2,1)}, bf16[1280,640]{1,0:T(8,128)(2,1)}, u32[]{:S(2)}, u32[]{:S(2)}) collective-permute-start(bf16[1280,640]{1,0:T(8,128)(2,1)} %slice_dynamic-update-slice_fusion), channel_id=1, source_target_pairs={{0,96},{32,0},{64,32},{96,64},{1,97},{33,1},{65,33},{97,65},{2,98}... | collective-permute-start | bytes 4915208 | tf_op jit(solution)/shard_map/ppermute | solution.py:17
  170.0 4.8 %copy-start.6 = (bf16[1280,640]{1,0:T(8,128)(2,1)}, bf16[1280,640]{1,0:T(8,128)(2,1)S(1)}, u32[]{:S(2)}) copy-start(bf16[1280,640]{1,0:T(8,128)(2,1)S(1)} %collective-permute-done.17) | copy-start | bytes 4915204
  170.0 4.7 %collective-permute-start = (s32[32]{0:T(128)S(1)}, s32[32]{0:T(128)S(1)}, u32[]{:S(2)}, u32[]{:S(2)}) collective-permute-start(s32[32]{0:T(128)S(1)} %copy-done.13), channel_id=1, source_target_pairs={{0,16},{16,0},{1,17},{17,1},{2,18},{18,2},{3,19},{19,3},{4,20},{20... | collective-permute-start | bytes 392 | tf_op jit(solution)/shard_map/ppermute | solution.py:17
  172.7 2.0 copy-start.8
  172.7 19.6 %collective-permute-start.18 = (bf16[640,640]{1,0:T(8,128)(2,1)}, bf16[640,640]{1,0:T(8,128)(2,1)S(1)}, u32[]{:S(2)}, u32[]{:S(2)}) collective-permute-start(bf16[640,640]{1,0:T(8,128)(2,1)} %slice.229), channel_id=1, source_target_pairs={{0,4},{4,8},{8,12},{12,0},{1,5},{5,9},{9,13},{13,1},{2,6},{6,10},{... | collective-permute-start | bytes 2457608 | tf_op jit(solution)/shard_map/ppermute | solution.py:17
  174.7 19.5 %collective-permute-start.16 = (bf16[640,640]{1,0:T(8,128)(2,1)}, bf16[640,640]{1,0:T(8,128)(2,1)}, u32[]{:S(2)}, u32[]{:S(2)}) collective-permute-start(bf16[640,640]{1,0:T(8,128)(2,1)} %slice.228), channel_id=1, source_target_pairs={{0,12},{4,0},{8,4},{12,8},{1,13},{5,1},{9,5},{13,9},{2,14},{6,2},{... | collective-permute-start | bytes 2457608 | tf_op jit(solution)/shard_map/ppermute | solution.py:17
  178.5 17.0 %copy-start.5 = (bf16[1280,640]{1,0:T(8,128)(2,1)S(1)}, bf16[1280,640]{1,0:T(8,128)(2,1)}, u32[]{:S(2)}) copy-start(bf16[1280,640]{1,0:T(8,128)(2,1)} %copy-done.4) | copy-start | bytes 4915204
  178.5 17.0 %copy-start.7 = (bf16[1280,640]{1,0:T(8,128)(2,1)S(1)}, bf16[1280,640]{1,0:T(8,128)(2,1)}, u32[]{:S(2)}) copy-start(bf16[1280,640]{1,0:T(8,128)(2,1)} %copy-done.6) | copy-start | bytes 4915204
  178.6 17.0 %copy-start.9 = (bf16[1280,640]{1,0:T(8,128)(2,1)S(1)}, bf16[1280,640]{1,0:T(8,128)(2,1)}, u32[]{:S(2)}) copy-start(bf16[1280,640]{1,0:T(8,128)(2,1)} %copy-done.8) | copy-start | bytes 4915204
  178.6 23.1 %collective-permute-start.11 = (bf16[640,640]{1,0:T(8,128)(2,1)S(1)}, bf16[640,640]{1,0:T(8,128)(2,1)S(1)}, u32[]{:S(2)}, u32[]{:S(2)}) collective-permute-start(bf16[640,640]{1,0:T(8,128)(2,1)S(1)} %slice.225), channel_id=1, source_target_pairs={{0,32},{32,64},{64,96},{96,0},{1,33},{33,65},{65,97},{97,1},{2,34}... | collective-permute-start | bytes 2457608 | tf_op jit(solution)/shard_map/ppermute | solution.py:17
  180.0 21.6 %collective-permute-start.9 = (bf16[640,640]{1,0:T(8,128)(2,1)S(1)}, bf16[640,640]{1,0:T(8,128)(2,1)S(1)}, u32[]{:S(2)}, u32[]{:S(2)}) collective-permute-start(bf16[640,640]{1,0:T(8,128)(2,1)S(1)} %slice.224), channel_id=1, source_target_pairs={{0,96},{32,0},{64,32},{96,64},{1,97},{33,1},{65,33},{97,65},{2,98}... | collective-permute-start | bytes 2457608 | tf_op jit(solution)/shard_map/ppermute | solution.py:17
  215.0 18.1 %copy-start.2 = (f32[128]{0:T(128)S(1)}, f32[128]{0:T(128)}, u32[]{:S(2)}) copy-start(f32[128]{0:T(128)} %param.11) | copy-start | bytes 1540
  215.0 18.1 %copy-start.3 = (f32[128]{0:T(128)S(1)}, f32[128]{0:T(128)}, u32[]{:S(2)}) copy-start(f32[128]{0:T(128)} %param.12) | copy-start | bytes 1540
  244.1 7.7 %copy-start.14 = (bf16[5120,1024]{1,0:T(8,128)(2,1)S(1)}, bf16[5120,1024]{1,0:T(8,128)(2,1)}, u32[]{:S(2)}) copy-start(bf16[5120,1024]{1,0:T(8,128)(2,1)} %all-gather.2.cloned.1.call-done) | copy-start | bytes 31457284
  249.3 13.1 %collective-permute-start.28 = (bf16[512,1280]{1,0:T(8,128)(2,1)S(1)}, bf16[512,1280]{1,0:T(8,128)(2,1)S(1)}, u32[]{:S(2)}, u32[]{:S(2)}) collective-permute-start(bf16[512,1280]{1,0:T(8,128)(2,1)S(1)} %slice.250), channel_id=1, source_target_pairs={{0,1},{1,0},{2,3},{3,2},{4,5},{5,4},{6,7},{7,6},{8,9},{9,8},{10,11... | collective-permute-start | bytes 3932168 | tf_op jit(solution)/shard_map/ppermute | solution.py:17
  255.0 9.3 %collective-permute-start.25 = (bf16[512,1280]{1,0:T(8,128)(2,1)S(1)}, bf16[512,1280]{1,0:T(8,128)(2,1)S(1)}, u32[]{:S(2)}, u32[]{:S(2)}) collective-permute-start(bf16[512,1280]{1,0:T(8,128)(2,1)S(1)} %slice.244), channel_id=1, source_target_pairs={{0,1},{1,0},{2,3},{3,2},{4,5},{5,4},{6,7},{7,6},{8,9},{9,8},{10,11... | collective-permute-start | bytes 3932168 | tf_op jit(solution)/shard_map/ppermute | solution.py:17
  258.4 7.6 %collective-permute-start.22 = (bf16[512,1280]{1,0:T(8,128)(2,1)S(1)}, bf16[512,1280]{1,0:T(8,128)(2,1)S(1)}, u32[]{:S(2)}, u32[]{:S(2)}) collective-permute-start(bf16[512,1280]{1,0:T(8,128)(2,1)S(1)} %slice.238), channel_id=1, source_target_pairs={{0,1},{1,0},{2,3},{3,2},{4,5},{5,4},{6,7},{7,6},{8,9},{9,8},{10,11... | collective-permute-start | bytes 3932168 | tf_op jit(solution)/shard_map/ppermute | solution.py:17
  262.2 4.3 %collective-permute-start.19 = (bf16[512,1280]{1,0:T(8,128)(2,1)S(1)}, bf16[512,1280]{1,0:T(8,128)(2,1)S(1)}, u32[]{:S(2)}, u32[]{:S(2)}) collective-permute-start(bf16[512,1280]{1,0:T(8,128)(2,1)S(1)} %slice.232), channel_id=1, source_target_pairs={{0,1},{1,0},{2,3},{3,2},{4,5},{5,4},{6,7},{7,6},{8,9},{9,8},{10,11... | collective-permute-start | bytes 3932168 | tf_op jit(solution)/shard_map/ppermute | solution.py:17
  262.7 8.9 %collective-permute-start.30 = (bf16[128,1280]{1,0:T(8,128)(2,1)S(1)}, bf16[128,1280]{1,0:T(8,128)(2,1)S(1)}, u32[]{:S(2)}, u32[]{:S(2)}) collective-permute-start(bf16[128,1280]{1,0:T(8,128)(2,1)S(1)} %get-tuple-element.22), channel_id=1, source_target_pairs={{0,18},{2,0},{16,2},{18,16},{1,19},{3,1},{17,3},{19,17},{4,22},{6,... | collective-permute-start | bytes 983048 | tf_op jit(solution)/shard_map/ppermute | solution.py:17
  262.8 10.1 %collective-permute-start.29 = (bf16[128,1280]{1,0:T(8,128)(2,1)S(1)}, bf16[128,1280]{1,0:T(8,128)(2,1)S(1)}, u32[]{:S(2)}, u32[]{:S(2)}) collective-permute-start(bf16[128,1280]{1,0:T(8,128)(2,1)S(1)} %get-tuple-element.21), channel_id=1, source_target_pairs={{0,2},{2,16},{16,18},{18,0},{1,3},{3,17},{17,19},{19,1},{4,6},{6,2... | collective-permute-start | bytes 983048 | tf_op jit(solution)/shard_map/ppermute | solution.py:17
  264.7 14.0 %collective-permute-start.27 = (bf16[128,1280]{1,0:T(8,128)(2,1)S(1)}, bf16[128,1280]{1,0:T(8,128)(2,1)S(1)}, u32[]{:S(2)}, u32[]{:S(2)}) collective-permute-start(bf16[128,1280]{1,0:T(8,128)(2,1)S(1)} %get-tuple-element.20), channel_id=1, source_target_pairs={{0,18},{2,0},{16,2},{18,16},{1,19},{3,1},{17,3},{19,17},{4,22},{6,... | collective-permute-start | bytes 983048 | tf_op jit(solution)/shard_map/ppermute | solution.py:17
  266.0 13.9 %collective-permute-start.26 = (bf16[128,1280]{1,0:T(8,128)(2,1)S(1)}, bf16[128,1280]{1,0:T(8,128)(2,1)S(1)}, u32[]{:S(2)}, u32[]{:S(2)}) collective-permute-start(bf16[128,1280]{1,0:T(8,128)(2,1)S(1)} %get-tuple-element.19), channel_id=1, source_target_pairs={{0,2},{2,16},{16,18},{18,0},{1,3},{3,17},{17,19},{19,1},{4,6},{6,2... | collective-permute-start | bytes 983048 | tf_op jit(solution)/shard_map/ppermute | solution.py:17
  266.6 19.1 %collective-permute-start.24 = (bf16[128,1280]{1,0:T(8,128)(2,1)S(1)}, bf16[128,1280]{1,0:T(8,128)(2,1)S(1)}, u32[]{:S(2)}, u32[]{:S(2)}) collective-permute-start(bf16[128,1280]{1,0:T(8,128)(2,1)S(1)} %get-tuple-element.18), channel_id=1, source_target_pairs={{0,18},{2,0},{16,2},{18,16},{1,19},{3,1},{17,3},{19,17},{4,22},{6,... | collective-permute-start | bytes 983048 | tf_op jit(solution)/shard_map/ppermute | solution.py:17
  271.6 15.3 %collective-permute-start.23 = (bf16[128,1280]{1,0:T(8,128)(2,1)S(1)}, bf16[128,1280]{1,0:T(8,128)(2,1)S(1)}, u32[]{:S(2)}, u32[]{:S(2)}) collective-permute-start(bf16[128,1280]{1,0:T(8,128)(2,1)S(1)} %get-tuple-element.17), channel_id=1, source_target_pairs={{0,2},{2,16},{16,18},{18,0},{1,3},{3,17},{17,19},{19,1},{4,6},{6,2... | collective-permute-start | bytes 983048 | tf_op jit(solution)/shard_map/ppermute | solution.py:17
  272.9 19.8 %collective-permute-start.21 = (bf16[128,1280]{1,0:T(8,128)(2,1)S(1)}, bf16[128,1280]{1,0:T(8,128)(2,1)S(1)}, u32[]{:S(2)}, u32[]{:S(2)}) collective-permute-start(bf16[128,1280]{1,0:T(8,128)(2,1)S(1)} %get-tuple-element.16), channel_id=1, source_target_pairs={{0,18},{2,0},{16,2},{18,16},{1,19},{3,1},{17,3},{19,17},{4,22},{6,... | collective-permute-start | bytes 983048 | tf_op jit(solution)/shard_map/ppermute | solution.py:17
  278.6 15.3 %collective-permute-start.20 = (bf16[128,1280]{1,0:T(8,128)(2,1)S(1)}, bf16[128,1280]{1,0:T(8,128)(2,1)S(1)}, u32[]{:S(2)}, u32[]{:S(2)}) collective-permute-start(bf16[128,1280]{1,0:T(8,128)(2,1)S(1)} %get-tuple-element.15), channel_id=1, source_target_pairs={{0,2},{2,16},{16,18},{18,0},{1,3},{3,17},{17,19},{19,1},{4,6},{6,2... | collective-permute-start | bytes 983048 | tf_op jit(solution)/shard_map/ppermute | solution.py:17
Sparse Core Ops, SparseCore 0:
  10.4 154.0 all-gather.1
where the time goes:
time: 306 us; the launch traced here: 303 us
  waiting for transfers between devices  148 us (48%)
  starting transfers between devices  48.5 us (16%)
  matrix products  45.9 us (15%)
  other arithmetic  16.6 us (5%)
  local copies, waits for them, and re-layouts  15.6 us (5%)
  between operations  14.1 us (5%)
  Pallas kernels  13.8 us (5%)
    ppermute x31, waiting for transfers between devices, shift(): lax.ppermute(value, axis, [(i, (i + steps) % size) for i in range(size)])  148 us
    ppermute x31, starting transfers between devices, shift(): lax.ppermute(value, axis, [(i, (i + steps) % size) for i in range(size)])  48.5 us
    dot_general x1, matrix products, per_device(): jnp.dot(all_rows, second_weights, preferred_element_type=jnp.float32)  18 us
    dot_general x4, matrix products, per_device(): lax.dot_general(attended, out_full[i * size:(i + 1) * size], contract, pr...  14.6 us
    dot_general x4, matrix products, per_device(): jnp.dot(all_rows[:, i * depth:(i + 1) * depth], part, preferred_element_t...  13.3 us
    pallas_call x1, Pallas kernels, attend(): pl.pallas_call(functools.partial(attend_kernel, splits), out_shape=jax.Sh...  10.9 us
    unnamed x39, local copies, waits for them, and re-layouts  7.45 us
  transfers between devices with their start and end apart: 32, of which 15 were waited for; matrix products, arithmetic and copies ran while one was open for 23% of the time, Pallas kernels for 5%

commit v1 on v0

v1 whole, which is shorter than its diff:
```python
import functools
import math

import jax
import jax.numpy as jnp
from jax import lax
from jax.experimental import pallas as pl
from jax.experimental.pallas import tpu as pltpu
from jax.sharding import Mesh, PartitionSpec as P

AXES = ("z", "xh", "y", "xl", "c")
SIZES = (4, 2, 4, 2, 2)
X = ("xh", "xl")
MIB = 1024 * 1024


def shift(value, axis, steps, size=4):
    return lax.ppermute(value, axis, [(i, (i + steps) % size) for i in range(size)])


def cross_shift(value, steps, first):
    pairs = []
    for z in range(4):
        for y in range(4):
            for c in range(2):
                along_y = (c == 0) == first
                tz, ty = (z, (y + steps) % 4) if along_y else ((z + steps) % 4, y)
                pairs.append(((z * 4 + y) * 2 + c, (tz * 4 + ty) * 2 + c))
    return lax.ppermute(value, ("z", "y", "c"), pairs)


def x_shift(value, steps):
    pairs = []
    for x in range(4):
        for c in range(2):
            pairs.append((x * 2 + c, (x + (steps if c == 0 else -steps)) % 4 * 2 + c))
    return lax.ppermute(value, X + ("c",), pairs)


def after(value, *others):
    return lax.optimization_barrier((value,) + others)[0]


def first_hop(block, move):
    return [block, move(block, -1), move(block, 2), move(block, 1)]


def norm_kernel(place, x_ref, gain_ref, left_ref, right_ref):
    z, y = place[0], place[1]
    x = x_ref[...].astype(jnp.float32)
    scale = lax.rsqrt(jnp.mean(x * x, axis=-1, keepdims=True) + 1e-06)
    width = x.shape[1] // 8
    piece = width // 4
    for block in range(8):
        part = x[:, block * width : (block + 1) * width]
        part = part * scale * gain_ref[:, block * width : (block + 1) * width]
        part = pltpu.roll(part, lax.rem(4 - y, 4) * piece, 1).astype(jnp.bfloat16)
        target = lax.rem(block // 2 - z + 4, 4) * 2 + block % 2
        at = pl.ds(pl.multiple_of(target * width, 128), width)

        @pl.when(pl.program_id(0) < 2)
        def _():
            left_ref[:, at] = part

        @pl.when(pl.program_id(0) >= 2)
        def _():
            right_ref[:, at] = part


def rolled_norm(states, gain, place):
    rows, width = states.shape
    step = 64
    return pl.pallas_call(
        norm_kernel,
        out_shape=[jax.ShapeDtypeStruct((rows // 2, width), jnp.bfloat16)] * 2,
        grid_spec=pltpu.PrefetchScalarGridSpec(
            num_scalar_prefetch=1,
            grid=(rows // step,),
            in_specs=[
                pl.BlockSpec((step, width), lambda i, p: (i, 0)),
                pl.BlockSpec((1, width), lambda i, p: (0, 0)),
            ],
            out_specs=[
                pl.BlockSpec((step, width), lambda i, p: (jnp.minimum(i, 1), 0)),
                pl.BlockSpec((step, width), lambda i, p: (jnp.maximum(i, 2) - 2, 0)),
            ],
        ),
        compiler_params=pltpu.CompilerParams(vmem_limit_bytes=32 * MIB),
        cost_estimate=pl.CostEstimate(flops=rows * width * 6, bytes_accessed=rows * width * 4, transcendentals=rows),
        name="norm",
    )(place, states, gain.reshape(1, width))


def by_core(c, first, second):
    return jnp.where(c == 0, first, second), jnp.where(c == 0, second, first)


def attend_rows(total, live, qgain, kgain, cosine, sine, o_ref):
    rows = total.shape[0]
    count = total.shape[1] // 128 - 2
    ones = jnp.ones((128, 128), jnp.bfloat16)
    stacked = jnp.concatenate([total[:, i * 128 : (i + 1) * 128] for i in range(count + 1)], axis=0)
    squares = jnp.dot((stacked * stacked).astype(jnp.bfloat16), ones, preferred_element_type=jnp.float32)
    scaled = stacked * lax.rsqrt(squares * (1.0 / 128.0) + 1e-06)
    prepared = []
    for h in range(count + 1):
        v = scaled[h * rows : (h + 1) * rows] * (qgain if h < count else kgain)
        prepared.append((v * cosine + pltpu.roll(v, 64, 1) * sine).astype(jnp.bfloat16))
    queries = jnp.concatenate(prepared[:count], axis=0)
    values = jnp.concatenate([total[:, (count + 1) * 128 :].astype(jnp.bfloat16), ones], axis=1)
    scores = lax.dot_general(
        queries, prepared[count], (((1,), (1,)), ((), ())), preferred_element_type=jnp.float32
    )
    i = lax.broadcasted_iota(jnp.int32, (rows, rows), 0)
    j = lax.broadcasted_iota(jnp.int32, (rows, rows), 1)
    allowed = (j <= i) & (j >= (i & ~31)) & (live > 0)
    weights = [
        jnp.where(allowed, jnp.exp(scores[h * rows : (h + 1) * rows] * (1.0 / math.sqrt(128.0))), 0.0)
        for h in range(count)
    ]
    weights = jnp.concatenate(weights, axis=0).astype(jnp.bfloat16)
    attended = jnp.dot(weights, values, preferred_element_type=jnp.float32)
    for h in range(count):
        part = attended[h * rows : (h + 1) * rows]
        o_ref[:, h * 128 : (h + 1) * 128] = (part[:, :128] / part[:, 128:]).astype(jnp.bfloat16)


def qkv_kernel(place, *refs):
    x_refs, (b0, b1, b2a, b2b, b3) = refs[:8], refs[8:13]
    rest_ref, live_ref, qgain_ref, kgain_ref, cos_ref, sin_ref, o_ref, w_ref, acc_ref, sems = refs[13:]
    y, core = place[1], place[2]
    step = pl.program_id(0)
    piece = b0.shape[0] // 8
    depth = piece * 8
    columns = b0.shape[1]

    def block(index, start):
        if index == 2:
            far = b2a.shape[0]
            return b2a.at[pl.ds(start, piece)] if start < far else b2b.at[pl.ds(start - far, piece)]
        return (b0, b1, None, b3)[index].at[pl.ds(start, piece)]

    def fetch(d, pick):
        for h in range(2):
            for e in range(4):
                target = w_ref.at[pl.ds(((d * 2 + h) * 4 + e) * piece, piece)]
                pltpu.make_async_copy(pick(h, e), target, sems.at[d]).start()

    for d in range(4):
        due = step == max(d - 1, 0)

        @pl.when(due & (core == 0))
        def _():
            fetch(d, lambda h, e: block(d, (e * 2 + h) * piece))

        @pl.when(due & (core != 0))
        def _():
            fetch(d, lambda h, e: block(e, (d * 2 + h) * piece))

    @pl.when(step == 0)
    def _():
        acc_ref[...] = jnp.zeros_like(acc_ref)

    @pl.when(step < 4)
    def _():
        at = pl.ds(pl.multiple_of(step * depth, 128), depth)
        pltpu.make_async_copy(w_ref.at[at], w_ref.at[at], sems.at[step]).wait()
        rest = jnp.concatenate(
            [
                rest_ref[pl.ds(pl.multiple_of((h * 4 + lax.rem(e + y, 4)) * piece, 32), piece), :]
                for h in range(2)
                for e in range(4)
            ],
            axis=0,
        )
        for g in range(2):
            x = jnp.concatenate([r[...] for r in x_refs[g * 4 : g * 4 + 4]], axis=0)
            rows = slice(g * 512, (g + 1) * 512)
            acc_ref[rows, :columns] += jnp.dot(x, w_ref[at, :], preferred_element_type=jnp.float32)
            acc_ref[rows, columns:] += jnp.dot(x, rest, preferred_element_type=jnp.float32)

    @pl.when(step >= 4)
    def _():
        attend_rows(
            acc_ref[pl.ds(pl.multiple_of((step - 4) * 128, 128), 128), :],
            live_ref[0],
            qgain_ref[...],
            kgain_ref[...],
            cos_ref[...],
            sin_ref[...],
            o_ref,
        )


def qkv_attend(place, tokens, blocks, rest, row_lengths, query_gain, key_norm_gain):
    sub, width = tokens[0].shape
    total = sub * len(tokens)
    head_width = query_gain.shape[0]
    slots = 32
    heads_width = blocks[0].shape[1]
    columns = heads_width + rest.shape[1]
    depth = width // 4
    half_width = head_width // 2
    freq_index = jnp.arange(half_width, dtype=jnp.float32)
    frequency = jnp.exp(freq_index * (-2.0 * math.log(1000000.0) / head_width))
    angles = jnp.arange(slots, dtype=jnp.float32)[:, None] * frequency[None, :]
    cosine, sine = jnp.cos(angles), jnp.sin(angles)
    cosine = jnp.tile(jnp.concatenate([cosine, cosine], axis=1), (sub // slots, 1))
    sine = jnp.tile(jnp.concatenate([-sine, sine], axis=1), (sub // slots, 1))
    live = (jnp.arange(slots, dtype=jnp.int32)[None, :] < row_lengths[:, None]).astype(jnp.int32)
    live = live.reshape(total // sub, 1, sub)

    def rest_index(i, p):
        return lax.rem(jnp.minimum(i, 3) + p[0], 4), 0

    fixed = [*blocks[:2], *blocks[2], blocks[3]]
    small = [query_gain.reshape(1, -1), key_norm_gain.reshape(1, -1), cosine, sine]
    return pl.pallas_call(
        qkv_kernel,
        out_shape=jax.ShapeDtypeStruct((total, heads_width), jnp.bfloat16),
        grid_spec=pltpu.PrefetchScalarGridSpec(
            num_scalar_prefetch=1,
            grid=(12,),
            in_specs=[pl.BlockSpec((sub, depth), lambda i, p: (0, jnp.minimum(i, 3)))] * len(tokens)
            + [pl.BlockSpec(memory_space=pl.ANY)] * len(fixed)
            + [pl.BlockSpec((depth, rest.shape[1]), rest_index)]
            + [pl.BlockSpec((1, 1, sub), lambda i, p: (jnp.maximum(i, 4) - 4, 0, 0))]
            + [pl.BlockSpec(a.shape, lambda i, p: (0, 0)) for a in small],
            out_specs=pl.BlockSpec((sub, heads_width), lambda i, p: (jnp.maximum(i, 4) - 4, 0)),
            scratch_shapes=[
                pltpu.VMEM((width, heads_width), jnp.bfloat16),
                pltpu.VMEM((total, columns), jnp.float32),
                pltpu.SemaphoreType.DMA((4,)),
            ],
        ),
        compiler_params=pltpu.CompilerParams(vmem_limit_bytes=44 * MIB),
        cost_estimate=pl.CostEstimate(
            flops=2 * total * width * columns, bytes_accessed=2 * (total + columns) * width, transcendentals=total * sub * 8
        ),
        name="qkv_attend",
    )(place, *tokens, *fixed, rest, live, *small)


def project(rows_ref, parts):
    weights = jnp.concatenate([p[...] for p in parts], axis=0) if len(parts) > 1 else parts[0][...]
    return lax.dot_general(
        rows_ref[...], weights, (((1,), (1,)), ((), ())), preferred_element_type=jnp.float32
    )


def give_kernel(split, rows_ref, *refs):
    parts, o_ref = refs[:-1], refs[-1]
    width = o_ref.shape[1] // 2
    o_ref[:, :width] = project(rows_ref, parts[:split]).astype(jnp.bfloat16)
    o_ref[:, width:] = project(rows_ref, parts[split:]).astype(jnp.bfloat16)


def keep_kernel(split, rows_ref, *refs):
    parts, (given_ref, own_ref, left_ref, right_ref) = refs[:-4], refs[-4:]
    width = own_ref.shape[1] // 2
    half = left_ref.shape[0]
    for at, weights in ((slice(0, width), parts[:split]), (slice(width, 2 * width), parts[split:])):
        chip = project(rows_ref, weights) + given_ref[:, at].astype(jnp.float32)
        own_ref[:, at] = chip[: 2 * half]
        left_ref[:, at] = chip[2 * half : 3 * half].astype(jnp.bfloat16)
        right_ref[:, at] = chip[3 * half :].astype(jnp.bfloat16)


def project_call(attended, even, odd, given=None):
    parts = [*even, *odd]
    rows, depth = attended.shape[0] // 2, attended.shape[1]
    width = sum(p.shape[0] for p in parts)
    keep = given is not None
    whole = lambda shape: pl.BlockSpec(shape, lambda i: (0, 0))
    out = [((rows, width), jnp.bfloat16)]
    if keep:
        out = [((rows // 2, width), jnp.float32)] + [((rows // 4, width), jnp.bfloat16)] * 2
    result = pl.pallas_call(
        functools.partial(keep_kernel if keep else give_kernel, len(even)),
        out_shape=[jax.ShapeDtypeStruct(*o) for o in out],
        grid=(1,),
        in_specs=[pl.BlockSpec((rows, depth), lambda i: (0 if keep else 1, 0))]
        + [whole(p.shape) for p in parts]
        + ([whole(given.shape)] if keep else []),
        out_specs=[whole(o[0]) for o in out],
        compiler_params=pltpu.CompilerParams(vmem_limit_bytes=32 * MIB),
        cost_estimate=pl.CostEstimate(
            flops=2 * rows * width * depth, bytes_accessed=2 * (rows + width) * depth + 2 * rows * width, transcendentals=0
        ),
        name="keep" if keep else "give",
    )(attended, *parts, *([given] if keep else []))
    return result if keep else result[0]


def finish_kernel(place, *refs):
    z, y = place[0], place[1]
    chips, firsts, seconds, o_ref = refs[0:4], refs[4:8], refs[8:12], refs[12]
    use_first = lax.rem(pl.program_id(0) + 1 + place[2], 2) == 0
    sums = []
    for chip, first, second in zip(chips, firsts, seconds):
        back = jnp.where(use_first, first[...], second[...]).astype(jnp.float32)
        sums.append(chip[...] + back)
    width = sums[0].shape[1] // 2
    piece = width // 4
    for d in range(4):
        other = jnp.concatenate(
            [sums[e][:, width + d * piece : width + (d + 1) * piece] for e in range(4)], axis=1
        )
        for h, part in enumerate((sums[d][:, :width], other)):
            part = pltpu.roll(part, y * piece, 1).astype(jnp.bfloat16)
            target = lax.rem(d + z, 4) * 2 + h
            o_ref[:, pl.ds(pl.multiple_of(target * width, 128), width)] = part


def finish(place, chips, firsts, seconds):
    rows, width = chips[0].shape
    half = rows // 2
    return pl.pallas_call(
        finish_kernel,
        out_shape=jax.ShapeDtypeStruct((rows, width * 4), jnp.bfloat16),
        grid_spec=pltpu.PrefetchScalarGridSpec(
            num_scalar_prefetch=1,
            grid=(2,),
            in_specs=[pl.BlockSpec((half, width), lambda i, p: (lax.rem(i + 1 + p[2], 2), 0))] * 4
            + [pl.BlockSpec((half, width), lambda i, p: (0, 0))] * 8,
            out_specs=pl.BlockSpec((half, width * 4), lambda i, p: (i, 0)),
        ),
        compiler_params=pltpu.CompilerParams(vmem_limit_bytes=40 * MIB),
        cost_estimate=pl.CostEstimate(flops=rows * width * 8, bytes_accessed=rows * width * 32, transcendentals=0),
        name="finish",
    )(place, *chips, *firsts, *seconds)


def per_device(
    states, norm_gain, query_gain, key_norm_gain, lengths, w_query, key_weight, value_weight, w_out
):
    z, y, xh, xl, c = (lax.axis_index(a) for a in ("z", "y", "xh", "xl", "c"))
    place = jnp.stack([z, y, c]).astype(jnp.int32)
    rows = states.shape[0]
    piece = w_query.shape[0]

    key_value = jnp.concatenate([key_weight, value_weight], axis=1)
    rest = lax.all_gather(key_value, ("z", "xh", "y"), axis=0, tiled=True)

    w_query = after(w_query, key_value)
    w_other = shift(w_query, "xh", 1, 2)
    out_other = shift(w_out, "xh", 1, 2)
    other_lengths = shift(lengths, "xh", 1, 2)
    left, right = rolled_norm(states, norm_gain, place)
    w_query, w_other, left, right = lax.optimization_barrier((w_query, w_other, left, right, other_lengths))[:4]
    w_pair = lax.dynamic_slice_in_dim(
        jnp.concatenate([w_query, w_other, w_query], axis=0), xh * piece, 2 * piece, axis=0
    )

    own = by_core(c, right, left)
    first_rows = x_shift(after(own[0], out_other), 1)
    second_rows = x_shift(after(own[1], first_rows), -1)
    mine = [*own, first_rows, second_rows]
    tokens = [*mine, *(shift(v, "c", 1, 2) for v in mine)]

    near = jnp.concatenate(first_hop(w_pair, lambda v, s: cross_shift(v, s, True)), axis=0)
    along = lambda v, s: cross_shift(v, s, False)
    before_, after_ = along(near, 1), along(near, -1)
    half = near.shape[0] // 2

    even = jnp.where(xh == 0, w_out, out_other)
    odd = jnp.where(xh == 0, out_other, w_out)
    even, odd = lax.optimization_barrier((even, odd, near))[:2]
    hops = {0: (even, odd)}
    for steps in (-1, 1, 2):
        hops[-steps % 4] = shift(even, "y", steps), shift(odd, "z", steps)
        even, odd, *_ = lax.optimization_barrier((even, odd, *hops[-steps % 4]))
    far = along(after_[:half], -1), along(before_[half:], 1)
    even_near, odd_near = (jnp.concatenate([hops[k][i] for k in range(4)], axis=0) for i in range(2))
    even_near, odd_near, rest, *far = lax.optimization_barrier((even_near, odd_near, rest, *far))
    blocks = [near, after_, tuple(far), before_]
    up_z, down_z = shift(even_near, "z", -1), shift(even_near, "z", 1)
    up_y, down_y = shift(odd_near, "y", -1), shift(odd_near, "y", 1)

    per = rows // 32
    hp = per // 2

    def prompt_lengths(core):
        own = lax.dynamic_slice_in_dim(lengths, (xl * 2 + core) * per, per)
        same = lax.dynamic_slice_in_dim(lengths, ((1 - xl) * 2 + core) * per, per)
        away = lax.dynamic_slice_in_dim(other_lengths, ((1 - xl) * 2 + core) * per, per)
        from_left = jnp.where(xl == 1, same, away)[hp:]
        from_right = jnp.where(xl == 0, same, away)[:hp]
        return [*by_core(core, own[hp:], own[:hp]), *by_core(core, from_left, from_right)]

    row_lengths = jnp.concatenate(prompt_lengths(c) + prompt_lengths(1 - c))
    attended = qkv_attend(place, tokens, blocks, rest, row_lengths, query_gain, key_norm_gain)

    up_z, down_z, up_y, down_y, attended = lax.optimization_barrier((up_z, down_z, up_y, down_y, attended))
    half = even_near.shape[0] // 2
    far_z = shift(up_z[:half], "z", -1), shift(down_z[half:], "z", 1)
    far_y = shift(up_y[:half], "y", -1), shift(down_y[half:], "y", 1)
    pieces = [((even_near,), (odd_near,)), ((up_z,), (up_y,)), (far_z, far_y), ((down_z,), (down_y,))]

    results = [None] * 4
    for k in (0, 1, 3, 2):
        given = shift(project_call(attended, *pieces[k]), "c", 1, 2)
        chip, first_back, second_back = project_call(attended, *pieces[k], given)
        results[k] = (chip, x_shift(first_back, -1), x_shift(second_back, 1))
    return finish(place, *zip(*results))


def solution(mesh):
    fine = Mesh(mesh.devices.reshape(SIZES), AXES)
    grp, tp = ("z", "xh", "y"), ("xl", "c")
    placed = (
        P(grp + tp, None),
        P(),
        P(),
        P(),
        P(grp),
        P(grp, tp),
        P(grp, tp),
        P(grp, tp),
        P(grp, tp),
    )
    return jax.shard_map(
        per_device, mesh=fine, in_specs=placed, out_specs=P(grp + tp, None), check_vma=False
    )
```

time: 306 us -> 238 us (0.78)
  waiting for transfers between devices: 148 us -> 87.1 us
  matrix products: 45.9 us -> 0 us
  Pallas kernels: 13.8 us -> 52 us
  starting transfers between devices: 48.5 us -> 66.6 us
  other arithmetic: 16.6 us -> 8.84 us
  local copies, waits for them, and re-layouts: 15.6 us -> 9.37 us
    ppermute x31 -> x25, waiting for transfers between devices: 148 us -> 26.4 us  [shift(): lax.ppermute(value, axis, [(i, (i + steps) % size) for i in range(size)])]
    ppermute x0 -> x17, waiting for transfers between devices: none -> 60.7 us  [the longest x10 32.4 us: x_shift(): return lax.ppermute(value, X + ('c',), pairs)]
    dot_general x9 -> x0, matrix products: 45.9 us -> none  [the longest x1 18 us: per_device(): jnp.dot(all_rows, second_weights, preferred_element_type=jnp.float32)]
    pallas_call x2 -> x11, Pallas kernels: 13.8 us -> 52 us  [the longest x1 28.4 us: qkv_attend(): pl.pallas_call(qkv_kernel, out_shape=jax.ShapeDtypeStruct((total, heads_w...]
    ppermute x0 -> x17, starting transfers between devices: none -> 23.4 us  [the longest x10 13.9 us: x_shift(): return lax.ppermute(value, X + ('c',), pairs)]
    concatenate x7 -> x5, other arithmetic: 13.6 us -> 5.7 us  [the longest x1 2.77 us: per_device(): jnp.concatenate(first_hop(w_pair, lambda v, s: cross_shift(v, s, True)),...]
    ppermute x31 -> x25, starting transfers between devices: 48.5 us -> 43.2 us  [shift(): lax.ppermute(value, axis, [(i, (i + steps) % size) for i in range(size)])]
    unnamed x39 -> x25, local copies, waits for them, and re-layouts: 7.45 us -> 4.05 us
  transfers between devices with their start and end apart: 32 -> 43, of which waited for: 15 -> 15; matrix products, arithmetic and copies ran while one was open for 23% -> 5% of each run, Pallas kernels for 5% -> 20%
where the time goes in v1:
time: 238 us
  waiting for transfers between devices  87.1 us (37%)
  starting transfers between devices  66.6 us (28%)
  Pallas kernels  52 us (22%)
  between operations  13.8 us (6%)
  local copies, waits for them, and re-layouts  9.37 us (4%)
  other arithmetic  8.84 us (4%)
    ppermute x25, starting transfers between devices, shift(): lax.ppermute(value, axis, [(i, (i + steps) % size) for i in range(size)])  43.2 us
    ppermute x10, waiting for transfers between devices, x_shift(): return lax.ppermute(value, X + ('c',), pairs)  32.4 us
    pallas_call x1, Pallas kernels, qkv_attend(): pl.pallas_call(qkv_kernel, out_shape=jax.ShapeDtypeStruct((total, heads_w...  28.4 us
    ppermute x7, waiting for transfers between devices, cross_shift(): return lax.ppermute(value, ('z', 'y', 'c'), pairs)  28.3 us
    ppermute x25, waiting for transfers between devices, shift(): lax.ppermute(value, axis, [(i, (i + steps) % size) for i in range(size)])  26.4 us
    pallas_call x8, Pallas kernels, project_call(): pl.pallas_call(functools.partial(keep_kernel if keep else give_kernel, le...  14.6 us
    ppermute x10, starting transfers between devices, x_shift(): return lax.ppermute(value, X + ('c',), pairs)  13.9 us
    ppermute x7, starting transfers between devices, cross_shift(): return lax.ppermute(value, ('z', 'y', 'c'), pairs)  9.43 us
  transfers between devices with their start and end apart: 43, of which 15 were waited for; matrix products, arithmetic and copies ran while one was open for 5% of the time, Pallas kernels for 20%

profile of v1, /device:TPU:1, one launch (start us, length us, event | category | flops | bytes accessed | tf_op | source)
XLA Modules:
  0.0 237.8 jit_solution(123932447586272296)
XLA Ops:
  8.1 3.7 %collective-permute-start.1 = (bf16[160,1024]{1,0:T(8,128)(2,1)}, bf16[160,1024]{1,0:T(8,128)(2,1)}, u32[]{:S(2)}, u32[]{:S(2)}) collective-permute-start(bf16[160,1024]{1,0:T(8,128)(2,1)} %param.14), channel_id=1, source_target_pairs={{0,16},{16,0},{1,17},{17,1},{2,18},{18,2},{3,19},{19,3},{4,20},{20... | collective-permute-start | bytes 983048 | tf_op jit(solution)/shard_map/ppermute | solution.py:18
  12.0 1.7 copy-done.1
  14.4 5.2 %norm.1 = (bf16[128,5120]{1,0:T(8,128)(2,1)S(1)}, bf16[128,5120]{1,0:T(8,128)(2,1)S(1)}) custom-call(s32[3]{0:T(128)S(1)} %pad_add_fusion.place, bf16[256,5120]{1,0:T(8,128)(2,1)S(1)} %copy-done.1, f32[1,5120]{1,0:T(1,128)S(1)} %bitcast.10), custom_call_target="tpu_custom_call" | custom-call | flops 7864320 | bytes 5242880 | tf_op jit(solution)/shard_map/norm/pallas_call | solution.py:73
  19.7 1.6 fusion.1
  21.3 1.8 collective-permute-start.5
  23.2 3.3 %collective-permute-start.4 = (bf16[320,1024]{1,0:T(8,128)(2,1)S(1)}, bf16[320,1024]{1,0:T(8,128)(2,1)}, u32[]{:S(2)}, u32[]{:S(2)}) collective-permute-start(bf16[320,1024]{1,0:T(8,128)(2,1)S(1)} %fusion.1), channel_id=1, source_target_pairs={{0,8},{1,65},{4,12},{5,69},{8,0},{9,73},{12,4},{13,77},{32,40},{33... | collective-permute-start | bytes 1966088 | tf_op jit(solution)/shard_map/ppermute | solution.py:29
  27.2 2.8 %collective-permute-start = (bf16[160,1024]{1,0:T(8,128)(2,1)}, bf16[160,1024]{1,0:T(8,128)(2,1)}, u32[]{:S(2)}, u32[]{:S(2)}) collective-permute-start(bf16[160,1024]{1,0:T(8,128)(2,1)} %param.17), channel_id=1, source_target_pairs={{0,16},{16,0},{1,17},{17,1},{2,18},{18,2},{3,19},{19,3},{4,20},{20... | collective-permute-start | bytes 983048 | tf_op jit(solution)/shard_map/ppermute | solution.py:18
  30.0 3.6 %collective-permute-done.5 = bf16[320,1024]{1,0:T(8,128)(2,1)} collective-permute-done((bf16[320,1024]{1,0:T(8,128)(2,1)S(1)}, bf16[320,1024]{1,0:T(8,128)(2,1)}, u32[]{:S(2)}, u32[]{:S(2)}) %collective-permute-start.5) | collective-permute-done | bytes 655392 | tf_op jit(solution)/shard_map/ppermute | solution.py:29
  33.6 8.2 %collective-permute-done.4 = bf16[320,1024]{1,0:T(8,128)(2,1)} collective-permute-done((bf16[320,1024]{1,0:T(8,128)(2,1)S(1)}, bf16[320,1024]{1,0:T(8,128)(2,1)}, u32[]{:S(2)}, u32[]{:S(2)}) %collective-permute-start.4) | collective-permute-done | bytes 655392 | tf_op jit(solution)/shard_map/ppermute | solution.py:29
  41.9 2.8 %pad_maximum_fusion.refs_8_ = bf16[1280,1024]{1,0:T(8,128)(2,1)} fusion(bf16[320,1024]{1,0:T(8,128)(2,1)} %collective-permute-done.5, bf16[320,1024]{1,0:T(8,128)(2,1)} %collective-permute-done.4, bf16[320,1024]{1,0:T(8,128)(2,1)} %collective-permute-done.3, bf16[320,1024]{1,0:T(8,128)(2,1)S(1)} %fusion.1), kind=kLoop, calls=%fused_computation | loop fusion | flops 10485760 | bytes 5242880 | tf_op jit(solution)/shard_map/concatenate | solution.py:361
  45.6 1.7 collective-permute-start.12
  47.3 1.7 broadcast_select_fusion
  49.0 2.5 %collective-permute-start.20 = (bf16[128,5120]{1,0:T(8,128)(2,1)}, bf16[128,5120]{1,0:T(8,128)(2,1)}, u32[]{:S(2)}, u32[]{:S(2)}) collective-permute-start(bf16[128,5120]{1,0:T(8,128)(2,1)} %get-tuple-element.57.refs_0_), channel_id=1, source_target_pairs={{0,2},{1,19},{2,16},{3,1},{16,18},{17,3},{18,0},{19,17},{4,6},{5,2... | collective-permute-start | bytes 3932168 | tf_op jit(solution)/shard_map/ppermute | solution.py:37
  51.5 17.2 %collective-permute-done.20.refs_2_ = bf16[128,5120]{1,0:T(8,128)(2,1)} collective-permute-done((bf16[128,5120]{1,0:T(8,128)(2,1)}, bf16[128,5120]{1,0:T(8,128)(2,1)}, u32[]{:S(2)}, u32[]{:S(2)}) %collective-permute-start.20) | collective-permute-done | bytes 1310752 | tf_op jit(solution)/shard_map/ppermute | solution.py:37
  69.5 9.4 %collective-permute-done.14.refs_12_ = bf16[1280,1024]{1,0:T(8,128)(2,1)} collective-permute-done((bf16[1280,1024]{1,0:T(8,128)(2,1)}, bf16[1280,1024]{1,0:T(8,128)(2,1)}, u32[]{:S(2)}, u32[]{:S(2)}) %collective-permute-start.14) | collective-permute-done | bytes 2621472 | tf_op jit(solution)/shard_map/ppermute | solution.py:29
  81.6 2.7 %collective-permute-start.6 = (bf16[160,1024]{1,0:T(8,128)(2,1)S(1)}, bf16[160,1024]{1,0:T(8,128)(2,1)S(1)}, u32[]{:S(2)}, u32[]{:S(2)}) collective-permute-start(bf16[160,1024]{1,0:T(8,128)(2,1)S(1)} %get-tuple-element.51), channel_id=1, source_target_pairs={{0,12},{4,0},{8,4},{12,8},{1,13},{5,1},{9,5},{13,9},{2,14},{6,2},{... | collective-permute-start | bytes 983048 | tf_op jit(solution)/shard_map/ppermute | solution.py:18
  84.3 2.3 collective-permute-start.7
  86.6 2.0 collective-permute-done.6
  88.7 2.6 %collective-permute-done.7 = bf16[160,1024]{1,0:T(8,128)(2,1)S(1)} collective-permute-done((bf16[160,1024]{1,0:T(8,128)(2,1)S(1)}, bf16[160,1024]{1,0:T(8,128)(2,1)S(1)}, u32[]{:S(2)}, u32[]{:S(2)}) %collective-permute-start.7) | collective-permute-done | bytes 327712 | tf_op jit(solution)/shard_map/ppermute | solution.py:18
  92.5 19.4 %collective-permute-done.8 = bf16[160,1024]{1,0:T(8,128)(2,1)S(1)} collective-permute-done((bf16[160,1024]{1,0:T(8,128)(2,1)S(1)}, bf16[160,1024]{1,0:T(8,128)(2,1)S(1)}, u32[]{:S(2)}, u32[]{:S(2)}) %collective-permute-start.8) | collective-permute-done | bytes 327712 | tf_op jit(solution)/shard_map/ppermute | solution.py:18
  112.6 2.2 collective-permute-start.11
  114.7 2.5 %slice.56 = bf16[640,1024]{1,0:T(8,128)(2,1)} slice(bf16[1280,1024]{1,0:T(8,128)(2,1)} %collective-permute-done.12.refs_9_), slice={[0:640], [0:1024]} | slice | bytes 2621440 | tf_op jit(solution)/shard_map/slice | solution.py:373
  119.5 4.3 %collective-permute-start.23 = (bf16[128,5120]{1,0:T(8,128)(2,1)}, bf16[128,5120]{1,0:T(8,128)(2,1)}, u32[]{:S(2)}, u32[]{:S(2)}) collective-permute-start(bf16[128,5120]{1,0:T(8,128)(2,1)} %get-tuple-element.58.refs_1_), channel_id=1, source_target_pairs={{0,1},{1,0},{2,3},{3,2},{4,5},{5,4},{6,7},{7,6},{8,9},{9,8},{10,11... | collective-permute-start | bytes 3932168 | tf_op jit(solution)/shard_map/ppermute | solution.py:18
  124.5 2.7 %collective-permute-start.22 = (bf16[128,5120]{1,0:T(8,128)(2,1)}, bf16[128,5120]{1,0:T(8,128)(2,1)}, u32[]{:S(2)}, u32[]{:S(2)}) collective-permute-start(bf16[128,5120]{1,0:T(8,128)(2,1)} %get-tuple-element.57.refs_0_), channel_id=1, source_target_pairs={{0,1},{1,0},{2,3},{3,2},{4,5},{5,4},{6,7},{7,6},{8,9},{9,8},{10,11... | collective-permute-start | bytes 3932168 | tf_op jit(solution)/shard_map/ppermute | solution.py:18
  130.0 7.0 %collective-permute-done.13.refs_10_ = bf16[640,1024]{1,0:T(8,128)(2,1)} collective-permute-done((bf16[640,1024]{1,0:T(8,128)(2,1)}, bf16[640,1024]{1,0:T(8,128)(2,1)}, u32[]{:S(2)}, u32[]{:S(2)}) %collective-permute-start.13) | collective-permute-done | bytes 1310752 | tf_op jit(solution)/shard_map/ppermute | solution.py:29
  137.0 2.7 %collective-permute-start.16 = (bf16[640,1024]{1,0:T(8,128)(2,1)S(1)}, bf16[640,1024]{1,0:T(8,128)(2,1)S(1)}, u32[]{:S(2)}, u32[]{:S(2)}) collective-permute-start(bf16[640,1024]{1,0:T(8,128)(2,1)S(1)} %pad_maximum_fusion.1.refs_0_), channel_id=1, source_target_pairs={{0,96},{32,0},{64,32},{96,64},{1,97},{33,1},{65,33},{97,65},{2,98}... | collective-permute-start | bytes 3932168 | tf_op jit(solution)/shard_map/ppermute | solution.py:18
  142.5 28.4 %qkv_attend.1.rows_ref = bf16[1024,1024]{1,0:T(8,128)(2,1)} custom-call(s32[3]{0:T(128)S(1)} %pad_add_fusion.place, bf16[128,5120]{1,0:T(8,128)(2,1)} %get-tuple-element.57.refs_0_, bf16[128,5120]{1,0:T(8,128)(2,1)} %get-tuple-element.58.refs_1_, bf16[128,5120]{1,0:T(8,128)(2,1)} %collective-permute-done.20.refs_2_, ...), custom_call_target="tpu_custom_call" | custom-call | flops 13421772800 | bytes 23592960 | tf_op jit(solution)/shard_map/qkv_attend/pallas_call | solution.py:218
  171.2 2.7 %collective-permute-start.30 = (bf16[320,1024]{1,0:T(8,128)(2,1)S(1)}, bf16[320,1024]{1,0:T(8,128)(2,1)S(1)}, u32[]{:S(2)}, u32[]{:S(2)}) collective-permute-start(bf16[320,1024]{1,0:T(8,128)(2,1)S(1)} %slice.54), channel_id=1, source_target_pairs={{0,12},{4,0},{8,4},{12,8},{1,13},{5,1},{9,5},{13,9},{2,14},{6,2},{... | collective-permute-start | bytes 1966088 | tf_op jit(solution)/shard_map/ppermute | solution.py:18
  174.0 2.7 %collective-permute-start.28 = (bf16[320,1024]{1,0:T(8,128)(2,1)S(1)}, bf16[320,1024]{1,0:T(8,128)(2,1)S(1)}, u32[]{:S(2)}, u32[]{:S(2)}) collective-permute-start(bf16[320,1024]{1,0:T(8,128)(2,1)S(1)} %slice.52), channel_id=1, source_target_pairs={{0,96},{32,0},{64,32},{96,64},{1,97},{33,1},{65,33},{97,65},{2,98}... | collective-permute-start | bytes 1966088 | tf_op jit(solution)/shard_map/ppermute | solution.py:18
  176.6 1.8 give.4
  178.5 4.2 %collective-permute-start.26 = (bf16[512,1280]{1,0:T(8,128)(2,1)S(1)}, bf16[512,1280]{1,0:T(8,128)(2,1)S(1)}, u32[]{:S(2)}, u32[]{:S(2)}) collective-permute-start(bf16[512,1280]{1,0:T(8,128)(2,1)S(1)} %give.4), channel_id=1, source_target_pairs={{0,1},{1,0},{2,3},{3,2},{4,5},{5,4},{6,7},{7,6},{8,9},{9,8},{10,11... | collective-permute-start | bytes 3932168 | tf_op jit(solution)/shard_map/ppermute | solution.py:18
  182.7 1.8 give.7
  185.4 3.9 %collective-permute-start.33 = (bf16[512,1280]{1,0:T(8,128)(2,1)S(1)}, bf16[512,1280]{1,0:T(8,128)(2,1)S(1)}, u32[]{:S(2)}, u32[]{:S(2)}) collective-permute-start(bf16[512,1280]{1,0:T(8,128)(2,1)S(1)} %give.7), channel_id=1, source_target_pairs={{0,1},{1,0},{2,3},{3,2},{4,5},{5,4},{6,7},{7,6},{8,9},{9,8},{10,11... | collective-permute-start | bytes 3932168 | tf_op jit(solution)/shard_map/ppermute | solution.py:18
  189.3 1.8 give.5
  191.3 1.8 give.6
  193.9 1.8 keep.4
  198.5 1.8 keep.7
  200.4 2.7 %collective-permute-start.41 = (bf16[128,1280]{1,0:T(8,128)(2,1)S(1)}, bf16[128,1280]{1,0:T(8,128)(2,1)S(1)}, u32[]{:S(2)}, u32[]{:S(2)}) collective-permute-start(bf16[128,1280]{1,0:T(8,128)(2,1)S(1)} %get-tuple-element.78), channel_id=1, source_target_pairs={{0,2},{1,19},{2,16},{3,1},{16,18},{17,3},{18,0},{19,17},{4,6},{5,2... | collective-permute-start | bytes 983048 | tf_op jit(solution)/shard_map/ppermute | solution.py:37
  203.1 1.8 keep.5
  205.0 1.8 keep.6
  206.8 2.7 %collective-permute-start.39 = (bf16[128,1280]{1,0:T(8,128)(2,1)S(1)}, bf16[128,1280]{1,0:T(8,128)(2,1)S(1)}, u32[]{:S(2)}, u32[]{:S(2)}) collective-permute-start(bf16[128,1280]{1,0:T(8,128)(2,1)S(1)} %get-tuple-element.76), channel_id=1, source_target_pairs={{0,2},{1,19},{2,16},{3,1},{16,18},{17,3},{18,0},{19,17},{4,6},{5,2... | collective-permute-start | bytes 983048 | tf_op jit(solution)/shard_map/ppermute | solution.py:37
  209.6 1.8 collective-permute-done.37.refs_7_
  211.4 2.2 collective-permute-start.40
  213.7 4.8 %collective-permute-done.35.refs_5_ = bf16[128,1280]{1,0:T(8,128)(2,1)S(1)} collective-permute-done((bf16[128,1280]{1,0:T(8,128)(2,1)S(1)}, bf16[128,1280]{1,0:T(8,128)(2,1)S(1)}, u32[]{:S(2)}, u32[]{:S(2)}) %collective-permute-start.35) | collective-permute-done | bytes 327712 | tf_op jit(solution)/shard_map/ppermute | solution.py:37
  218.4 2.3 collective-permute-done.39.refs_9_
  220.7 4.8 %collective-permute-done.36.refs_6_ = bf16[128,1280]{1,0:T(8,128)(2,1)S(1)} collective-permute-done((bf16[128,1280]{1,0:T(8,128)(2,1)S(1)}, bf16[128,1280]{1,0:T(8,128)(2,1)S(1)}, u32[]{:S(2)}, u32[]{:S(2)}) %collective-permute-start.36) | collective-permute-done | bytes 327712 | tf_op jit(solution)/shard_map/ppermute | solution.py:37
  225.4 1.7 collective-permute-done.40.refs_10_
  227.1 3.8 %finish.1 = bf16[256,5120]{1,0:T(8,128)(2,1)} custom-call(s32[3]{0:T(128)S(1)} %pad_add_fusion.place, f32[256,1280]{1,0:T(8,128)S(1)} %get-tuple-element.63.refs_0_, f32[256,1280]{1,0:T(8,128)S(1)} %get-tuple-element.66.refs_1_, f32[256,1280]{1,0:T(8,128)S(1)} %get-tuple-element.69.refs_2_, f32[256,1280]{1,0:T(8,128)S(1)} %get-tuple-element.70.refs_3_, ...), custom_call_target="tpu_custom_call" | custom-call | flops 2621440 | bytes 10485760 | tf_op jit(solution)/shard_map/finish/pallas_call | solution.py:318
  (104 shorter events, 23.0 us)
Async XLA Ops:
  6.5 130.5 %all-gather.2.cloned.1.call-start = ((), (), s32[]{:S(2)}) async-start(), calls=%async_computation | async-start | bytes 2703360 | tf_op jit(solution)/shard_map/all_gather | solution.py:343
  8.1 11.5 %copy-start.10 = (bf16[160,256]{1,0:T(8,128)(2,1)}, bf16[160,256]{1,0:T(8,128)(2,1)S(1)}, u32[]{:S(2)}) copy-start(bf16[160,256]{1,0:T(8,128)(2,1)S(1)} %constant_dynamic-update-slice_fusion) | copy-start | bytes 245764
  8.1 11.6 %collective-permute-start.1 = (bf16[160,1024]{1,0:T(8,128)(2,1)}, bf16[160,1024]{1,0:T(8,128)(2,1)}, u32[]{:S(2)}, u32[]{:S(2)}) collective-permute-start(bf16[160,1024]{1,0:T(8,128)(2,1)} %param.14), channel_id=1, source_target_pairs={{0,16},{16,0},{1,17},{17,1},{2,18},{18,2},{3,19},{19,3},{4,20},{20... | collective-permute-start | bytes 983048 | tf_op jit(solution)/shard_map/ppermute | solution.py:18
  11.8 7.9 %collective-permute-start.2 = (s32[32]{0:T(128)}, s32[32]{0:T(128)S(1)}, u32[]{:S(2)}, u32[]{:S(2)}) collective-permute-start(s32[32]{0:T(128)} %param.13), channel_id=1, source_target_pairs={{0,16},{16,0},{1,17},{17,1},{2,18},{18,2},{3,19},{19,3},{4,20},{20... | collective-permute-start | bytes 392 | tf_op jit(solution)/shard_map/ppermute | solution.py:18
  21.3 12.3 %collective-permute-start.5 = (bf16[320,1024]{1,0:T(8,128)(2,1)S(1)}, bf16[320,1024]{1,0:T(8,128)(2,1)}, u32[]{:S(2)}, u32[]{:S(2)}) collective-permute-start(bf16[320,1024]{1,0:T(8,128)(2,1)S(1)} %fusion.1), channel_id=1, source_target_pairs={{0,4},{1,33},{4,8},{5,37},{8,12},{9,41},{12,0},{13,45},{32,36},{33... | collective-permute-start | bytes 1966088 | tf_op jit(solution)/shard_map/ppermute | solution.py:29
  23.2 18.7 %collective-permute-start.4 = (bf16[320,1024]{1,0:T(8,128)(2,1)S(1)}, bf16[320,1024]{1,0:T(8,128)(2,1)}, u32[]{:S(2)}, u32[]{:S(2)}) collective-permute-start(bf16[320,1024]{1,0:T(8,128)(2,1)S(1)} %fusion.1), channel_id=1, source_target_pairs={{0,8},{1,65},{4,12},{5,69},{8,0},{9,73},{12,4},{13,77},{32,40},{33... | collective-permute-start | bytes 1966088 | tf_op jit(solution)/shard_map/ppermute | solution.py:29
  26.5 15.4 %collective-permute-start.3 = (bf16[320,1024]{1,0:T(8,128)(2,1)S(1)}, bf16[320,1024]{1,0:T(8,128)(2,1)}, u32[]{:S(2)}, u32[]{:S(2)}) collective-permute-start(bf16[320,1024]{1,0:T(8,128)(2,1)S(1)} %fusion.1), channel_id=1, source_target_pairs={{0,12},{1,97},{4,0},{5,101},{8,4},{9,105},{12,8},{13,109},{32,44},... | collective-permute-start | bytes 1966088 | tf_op jit(solution)/shard_map/ppermute | solution.py:29
  27.2 21.8 %collective-permute-start = (bf16[160,1024]{1,0:T(8,128)(2,1)}, bf16[160,1024]{1,0:T(8,128)(2,1)}, u32[]{:S(2)}, u32[]{:S(2)}) collective-permute-start(bf16[160,1024]{1,0:T(8,128)(2,1)} %param.17), channel_id=1, source_target_pairs={{0,16},{16,0},{1,17},{17,1},{2,18},{18,2},{3,19},{19,3},{4,20},{20... | collective-permute-start | bytes 983048 | tf_op jit(solution)/shard_map/ppermute | solution.py:18
  44.6 34.4 %collective-permute-start.14 = (bf16[1280,1024]{1,0:T(8,128)(2,1)}, bf16[1280,1024]{1,0:T(8,128)(2,1)}, u32[]{:S(2)}, u32[]{:S(2)}) collective-permute-start(bf16[1280,1024]{1,0:T(8,128)(2,1)} %pad_maximum_fusion.refs_8_), channel_id=1, source_target_pairs={{0,32},{1,5},{4,36},{5,9},{8,40},{9,13},{12,44},{13,1},{32,64},{33... | collective-permute-start | bytes 7864328 | tf_op jit(solution)/shard_map/ppermute | solution.py:29
  45.6 69.1 %collective-permute-start.12 = (bf16[1280,1024]{1,0:T(8,128)(2,1)}, bf16[1280,1024]{1,0:T(8,128)(2,1)}, u32[]{:S(2)}, u32[]{:S(2)}) collective-permute-start(bf16[1280,1024]{1,0:T(8,128)(2,1)} %pad_maximum_fusion.refs_8_), channel_id=1, source_target_pairs={{0,96},{1,13},{4,100},{5,1},{8,104},{9,5},{12,108},{13,9},{32,0},{... | collective-permute-start | bytes 7864328 | tf_op jit(solution)/shard_map/ppermute | solution.py:29
  49.0 19.7 %collective-permute-start.20 = (bf16[128,5120]{1,0:T(8,128)(2,1)}, bf16[128,5120]{1,0:T(8,128)(2,1)}, u32[]{:S(2)}, u32[]{:S(2)}) collective-permute-start(bf16[128,5120]{1,0:T(8,128)(2,1)} %get-tuple-element.57.refs_0_), channel_id=1, source_target_pairs={{0,2},{1,19},{2,16},{3,1},{16,18},{17,3},{18,0},{19,17},{4,6},{5,2... | collective-permute-start | bytes 3932168 | tf_op jit(solution)/shard_map/ppermute | solution.py:37
  68.7 58.6 %collective-permute-start.21 = (bf16[128,5120]{1,0:T(8,128)(2,1)}, bf16[128,5120]{1,0:T(8,128)(2,1)}, u32[]{:S(2)}, u32[]{:S(2)}) collective-permute-start(bf16[128,5120]{1,0:T(8,128)(2,1)} %get-tuple-element.58.refs_1_), channel_id=1, source_target_pairs={{0,18},{1,3},{2,0},{3,17},{16,2},{17,19},{18,16},{19,1},{4,22},{5,... | collective-permute-start | bytes 3932168 | tf_op jit(solution)/shard_map/ppermute | solution.py:37
  69.5 10.9 %copy-start.9 = (bf16[160,1024]{1,0:T(8,128)(2,1)S(1)}, bf16[160,1024]{1,0:T(8,128)(2,1)}, u32[]{:S(2)}) copy-start(bf16[160,1024]{1,0:T(8,128)(2,1)} %param.17) | copy-start | bytes 983044
  80.4 47.0 %collective-permute-start.15 = (bf16[640,1024]{1,0:T(8,128)(2,1)S(1)}, bf16[640,1024]{1,0:T(8,128)(2,1)}, u32[]{:S(2)}, u32[]{:S(2)}) collective-permute-start(bf16[640,1024]{1,0:T(8,128)(2,1)S(1)} %slice.57), channel_id=1, source_target_pairs={{0,32},{1,5},{4,36},{5,9},{8,40},{9,13},{12,44},{13,1},{32,64},{33... | collective-permute-start | bytes 3932168 | tf_op jit(solution)/shard_map/ppermute | solution.py:29
  81.5 46.6 %copy-start.11 = (s32[32]{0:T(128)S(1)}, s32[32]{0:T(128)}, u32[]{:S(2)}) copy-start(s32[32]{0:T(128)} %param.13) | copy-start | bytes 388
  81.6 7.1 %collective-permute-start.6 = (bf16[160,1024]{1,0:T(8,128)(2,1)S(1)}, bf16[160,1024]{1,0:T(8,128)(2,1)S(1)}, u32[]{:S(2)}, u32[]{:S(2)}) collective-permute-start(bf16[160,1024]{1,0:T(8,128)(2,1)S(1)} %get-tuple-element.51), channel_id=1, source_target_pairs={{0,12},{4,0},{8,4},{12,8},{1,13},{5,1},{9,5},{13,9},{2,14},{6,2},{... | collective-permute-start | bytes 983048 | tf_op jit(solution)/shard_map/ppermute | solution.py:18
  84.3 7.0 %collective-permute-start.7 = (bf16[160,1024]{1,0:T(8,128)(2,1)S(1)}, bf16[160,1024]{1,0:T(8,128)(2,1)S(1)}, u32[]{:S(2)}, u32[]{:S(2)}) collective-permute-start(bf16[160,1024]{1,0:T(8,128)(2,1)S(1)} %get-tuple-element.52), channel_id=1, source_target_pairs={{0,96},{32,0},{64,32},{96,64},{1,97},{33,1},{65,33},{97,65},{2,98}... | collective-permute-start | bytes 983048 | tf_op jit(solution)/shard_map/ppermute | solution.py:18
  91.3 20.7 %collective-permute-start.8 = (bf16[160,1024]{1,0:T(8,128)(2,1)S(1)}, bf16[160,1024]{1,0:T(8,128)(2,1)S(1)}, u32[]{:S(2)}, u32[]{:S(2)}) collective-permute-start(bf16[160,1024]{1,0:T(8,128)(2,1)S(1)} %get-tuple-element.51), channel_id=1, source_target_pairs={{0,4},{4,8},{8,12},{12,0},{1,5},{5,9},{9,13},{13,1},{2,6},{6,10},{... | collective-permute-start | bytes 983048 | tf_op jit(solution)/shard_map/ppermute | solution.py:18
  91.3 20.7 %collective-permute-start.9 = (bf16[160,1024]{1,0:T(8,128)(2,1)S(1)}, bf16[160,1024]{1,0:T(8,128)(2,1)S(1)}, u32[]{:S(2)}, u32[]{:S(2)}) collective-permute-start(bf16[160,1024]{1,0:T(8,128)(2,1)S(1)} %get-tuple-element.52), channel_id=1, source_target_pairs={{0,32},{32,64},{64,96},{96,0},{1,33},{33,65},{65,97},{97,1},{2,34}... | collective-permute-start | bytes 983048 | tf_op jit(solution)/shard_map/ppermute | solution.py:18
  111.9 7.5 %collective-permute-start.10 = (bf16[160,1024]{1,0:T(8,128)(2,1)S(1)}, bf16[160,1024]{1,0:T(8,128)(2,1)}, u32[]{:S(2)}, u32[]{:S(2)}) collective-permute-start(bf16[160,1024]{1,0:T(8,128)(2,1)S(1)} %get-tuple-element.51), channel_id=1, source_target_pairs={{0,8},{4,12},{8,0},{12,4},{1,9},{5,13},{9,1},{13,5},{2,10},{6,14},... | collective-permute-start | bytes 983048 | tf_op jit(solution)/shard_map/ppermute | solution.py:18
  112.6 11.2 %collective-permute-start.11 = (bf16[160,1024]{1,0:T(8,128)(2,1)S(1)}, bf16[160,1024]{1,0:T(8,128)(2,1)S(1)}, u32[]{:S(2)}, u32[]{:S(2)}) collective-permute-start(bf16[160,1024]{1,0:T(8,128)(2,1)S(1)} %get-tuple-element.52), channel_id=1, source_target_pairs={{0,64},{32,96},{64,0},{96,32},{1,65},{33,97},{65,1},{97,33},{2,66}... | collective-permute-start | bytes 983048 | tf_op jit(solution)/shard_map/ppermute | solution.py:18
  117.3 19.8 %collective-permute-start.13 = (bf16[640,1024]{1,0:T(8,128)(2,1)}, bf16[640,1024]{1,0:T(8,128)(2,1)}, u32[]{:S(2)}, u32[]{:S(2)}) collective-permute-start(bf16[640,1024]{1,0:T(8,128)(2,1)} %slice.56), channel_id=1, source_target_pairs={{0,96},{1,13},{4,100},{5,1},{8,104},{9,5},{12,108},{13,9},{32,0},{... | collective-permute-start | bytes 3932168 | tf_op jit(solution)/shard_map/ppermute | solution.py:29
  119.5 17.6 %collective-permute-start.23 = (bf16[128,5120]{1,0:T(8,128)(2,1)}, bf16[128,5120]{1,0:T(8,128)(2,1)}, u32[]{:S(2)}, u32[]{:S(2)}) collective-permute-start(bf16[128,5120]{1,0:T(8,128)(2,1)} %get-tuple-element.58.refs_1_), channel_id=1, source_target_pairs={{0,1},{1,0},{2,3},{3,2},{4,5},{5,4},{6,7},{7,6},{8,9},{9,8},{10,11... | collective-permute-start | bytes 3932168 | tf_op jit(solution)/shard_map/ppermute | solution.py:18
  124.5 15.2 %collective-permute-start.22 = (bf16[128,5120]{1,0:T(8,128)(2,1)}, bf16[128,5120]{1,0:T(8,128)(2,1)}, u32[]{:S(2)}, u32[]{:S(2)}) collective-permute-start(bf16[128,5120]{1,0:T(8,128)(2,1)} %get-tuple-element.57.refs_0_), channel_id=1, source_target_pairs={{0,1},{1,0},{2,3},{3,2},{4,5},{5,4},{6,7},{7,6},{8,9},{9,8},{10,11... | collective-permute-start | bytes 3932168 | tf_op jit(solution)/shard_map/ppermute | solution.py:18
  127.3 13.7 %collective-permute-start.24 = (bf16[128,5120]{1,0:T(8,128)(2,1)}, bf16[128,5120]{1,0:T(8,128)(2,1)}, u32[]{:S(2)}, u32[]{:S(2)}) collective-permute-start(bf16[128,5120]{1,0:T(8,128)(2,1)} %collective-permute-done.20.refs_2_), channel_id=1, source_target_pairs={{0,1},{1,0},{2,3},{3,2},{4,5},{5,4},{6,7},{7,6},{8,9},{9,8},{10,11... | collective-permute-start | bytes 3932168 | tf_op jit(solution)/shard_map/ppermute | solution.py:18
  127.4 15.0 %collective-permute-start.25 = (bf16[128,5120]{1,0:T(8,128)(2,1)}, bf16[128,5120]{1,0:T(8,128)(2,1)}, u32[]{:S(2)}, u32[]{:S(2)}) collective-permute-start(bf16[128,5120]{1,0:T(8,128)(2,1)} %collective-permute-done.21.refs_3_), channel_id=1, source_target_pairs={{0,1},{1,0},{2,3},{3,2},{4,5},{5,4},{6,7},{7,6},{8,9},{9,8},{10,11... | collective-permute-start | bytes 3932168 | tf_op jit(solution)/shard_map/ppermute | solution.py:18
  129.9 12.6 %copy-start.3 = (f32[128]{0:T(128)S(1)}, f32[128]{0:T(128)}, u32[]{:S(2)}) copy-start(f32[128]{0:T(128)} %param.11) | copy-start | bytes 1540
  129.9 12.6 %copy-start.4 = (f32[128]{0:T(128)S(1)}, f32[128]{0:T(128)}, u32[]{:S(2)}) copy-start(f32[128]{0:T(128)} %param.12) | copy-start | bytes 1540
  137.0 33.8 %collective-permute-start.17 = (bf16[640,1024]{1,0:T(8,128)(2,1)S(1)}, bf16[640,1024]{1,0:T(8,128)(2,1)S(1)}, u32[]{:S(2)}, u32[]{:S(2)}) collective-permute-start(bf16[640,1024]{1,0:T(8,128)(2,1)S(1)} %pad_maximum_fusion.1.refs_0_), channel_id=1, source_target_pairs={{0,32},{32,64},{64,96},{96,0},{1,33},{33,65},{65,97},{97,1},{2,34}... | collective-permute-start | bytes 3932168 | tf_op jit(solution)/shard_map/ppermute | solution.py:18
  137.0 33.8 %collective-permute-start.16 = (bf16[640,1024]{1,0:T(8,128)(2,1)S(1)}, bf16[640,1024]{1,0:T(8,128)(2,1)S(1)}, u32[]{:S(2)}, u32[]{:S(2)}) collective-permute-start(bf16[640,1024]{1,0:T(8,128)(2,1)S(1)} %pad_maximum_fusion.1.refs_0_), channel_id=1, source_target_pairs={{0,96},{32,0},{64,32},{96,64},{1,97},{33,1},{65,33},{97,65},{2,98}... | collective-permute-start | bytes 3932168 | tf_op jit(solution)/shard_map/ppermute | solution.py:18
  139.7 31.1 %collective-permute-start.19 = (bf16[640,1024]{1,0:T(8,128)(2,1)S(1)}, bf16[640,1024]{1,0:T(8,128)(2,1)S(1)}, u32[]{:S(2)}, u32[]{:S(2)}) collective-permute-start(bf16[640,1024]{1,0:T(8,128)(2,1)S(1)} %pad_maximum_fusion.2.refs_1_), channel_id=1, source_target_pairs={{0,4},{4,8},{8,12},{12,0},{1,5},{5,9},{9,13},{13,1},{2,6},{6,10},{... | collective-permute-start | bytes 3932168 | tf_op jit(solution)/shard_map/ppermute | solution.py:18
  140.9 29.9 %collective-permute-start.18 = (bf16[640,1024]{1,0:T(8,128)(2,1)S(1)}, bf16[640,1024]{1,0:T(8,128)(2,1)S(1)}, u32[]{:S(2)}, u32[]{:S(2)}) collective-permute-start(bf16[640,1024]{1,0:T(8,128)(2,1)S(1)} %pad_maximum_fusion.2.refs_1_), channel_id=1, source_target_pairs={{0,12},{4,0},{8,4},{12,8},{1,13},{5,1},{9,5},{13,9},{2,14},{6,2},{... | collective-permute-start | bytes 3932168 | tf_op jit(solution)/shard_map/ppermute | solution.py:18
  170.9 14.5 %collective-permute-start.31 = (bf16[320,1024]{1,0:T(8,128)(2,1)S(1)}, bf16[320,1024]{1,0:T(8,128)(2,1)S(1)}, u32[]{:S(2)}, u32[]{:S(2)}) collective-permute-start(bf16[320,1024]{1,0:T(8,128)(2,1)S(1)} %slice.55), channel_id=1, source_target_pairs={{0,4},{4,8},{8,12},{12,0},{1,5},{5,9},{9,13},{13,1},{2,6},{6,10},{... | collective-permute-start | bytes 1966088 | tf_op jit(solution)/shard_map/ppermute | solution.py:18
  171.1 20.1 %collective-permute-start.29 = (bf16[320,1024]{1,0:T(8,128)(2,1)S(1)}, bf16[320,1024]{1,0:T(8,128)(2,1)S(1)}, u32[]{:S(2)}, u32[]{:S(2)}) collective-permute-start(bf16[320,1024]{1,0:T(8,128)(2,1)S(1)} %slice.53), channel_id=1, source_target_pairs={{0,32},{32,64},{64,96},{96,0},{1,33},{33,65},{65,97},{97,1},{2,34}... | collective-permute-start | bytes 1966088 | tf_op jit(solution)/shard_map/ppermute | solution.py:18
  171.2 20.0 %collective-permute-start.30 = (bf16[320,1024]{1,0:T(8,128)(2,1)S(1)}, bf16[320,1024]{1,0:T(8,128)(2,1)S(1)}, u32[]{:S(2)}, u32[]{:S(2)}) collective-permute-start(bf16[320,1024]{1,0:T(8,128)(2,1)S(1)} %slice.54), channel_id=1, source_target_pairs={{0,12},{4,0},{8,4},{12,8},{1,13},{5,1},{9,5},{13,9},{2,14},{6,2},{... | collective-permute-start | bytes 1966088 | tf_op jit(solution)/shard_map/ppermute | solution.py:18
  174.0 17.3 %collective-permute-start.28 = (bf16[320,1024]{1,0:T(8,128)(2,1)S(1)}, bf16[320,1024]{1,0:T(8,128)(2,1)S(1)}, u32[]{:S(2)}, u32[]{:S(2)}) collective-permute-start(bf16[320,1024]{1,0:T(8,128)(2,1)S(1)} %slice.52), channel_id=1, source_target_pairs={{0,96},{32,0},{64,32},{96,64},{1,97},{33,1},{65,33},{97,65},{2,98}... | collective-permute-start | bytes 1966088 | tf_op jit(solution)/shard_map/ppermute | solution.py:18
  178.5 15.5 %collective-permute-start.26 = (bf16[512,1280]{1,0:T(8,128)(2,1)S(1)}, bf16[512,1280]{1,0:T(8,128)(2,1)S(1)}, u32[]{:S(2)}, u32[]{:S(2)}) collective-permute-start(bf16[512,1280]{1,0:T(8,128)(2,1)S(1)} %give.4), channel_id=1, source_target_pairs={{0,1},{1,0},{2,3},{3,2},{4,5},{5,4},{6,7},{7,6},{8,9},{9,8},{10,11... | collective-permute-start | bytes 3932168 | tf_op jit(solution)/shard_map/ppermute | solution.py:18
  185.4 13.1 %collective-permute-start.33 = (bf16[512,1280]{1,0:T(8,128)(2,1)S(1)}, bf16[512,1280]{1,0:T(8,128)(2,1)S(1)}, u32[]{:S(2)}, u32[]{:S(2)}) collective-permute-start(bf16[512,1280]{1,0:T(8,128)(2,1)S(1)} %give.7), channel_id=1, source_target_pairs={{0,1},{1,0},{2,3},{3,2},{4,5},{5,4},{6,7},{7,6},{8,9},{9,8},{10,11... | collective-permute-start | bytes 3932168 | tf_op jit(solution)/shard_map/ppermute | solution.py:18
  191.2 9.2 %collective-permute-start.27 = (bf16[512,1280]{1,0:T(8,128)(2,1)S(1)}, bf16[512,1280]{1,0:T(8,128)(2,1)S(1)}, u32[]{:S(2)}, u32[]{:S(2)}) collective-permute-start(bf16[512,1280]{1,0:T(8,128)(2,1)S(1)} %give.5), channel_id=1, source_target_pairs={{0,1},{1,0},{2,3},{3,2},{4,5},{5,4},{6,7},{7,6},{8,9},{9,8},{10,11... | collective-permute-start | bytes 3932168 | tf_op jit(solution)/shard_map/ppermute | solution.py:18
  193.1 11.8 %collective-permute-start.32 = (bf16[512,1280]{1,0:T(8,128)(2,1)S(1)}, bf16[512,1280]{1,0:T(8,128)(2,1)S(1)}, u32[]{:S(2)}, u32[]{:S(2)}) collective-permute-start(bf16[512,1280]{1,0:T(8,128)(2,1)S(1)} %give.6), channel_id=1, source_target_pairs={{0,1},{1,0},{2,3},{3,2},{4,5},{5,4},{6,7},{7,6},{8,9},{9,8},{10,11... | collective-permute-start | bytes 3932168 | tf_op jit(solution)/shard_map/ppermute | solution.py:18
  195.7 11.1 %collective-permute-start.34 = (bf16[128,1280]{1,0:T(8,128)(2,1)S(1)}, bf16[128,1280]{1,0:T(8,128)(2,1)S(1)}, u32[]{:S(2)}, u32[]{:S(2)}) collective-permute-start(bf16[128,1280]{1,0:T(8,128)(2,1)S(1)} %get-tuple-element.71), channel_id=1, source_target_pairs={{0,18},{1,3},{2,0},{3,17},{16,2},{17,19},{18,16},{19,1},{4,22},{5,... | collective-permute-start | bytes 983048 | tf_op jit(solution)/shard_map/ppermute | solution.py:37
  197.0 12.6 %collective-permute-start.38 = (bf16[128,1280]{1,0:T(8,128)(2,1)S(1)}, bf16[128,1280]{1,0:T(8,128)(2,1)S(1)}, u32[]{:S(2)}, u32[]{:S(2)}) collective-permute-start(bf16[128,1280]{1,0:T(8,128)(2,1)S(1)} %get-tuple-element.75), channel_id=1, source_target_pairs={{0,2},{1,19},{2,16},{3,1},{16,18},{17,3},{18,0},{19,17},{4,6},{5,2... | collective-permute-start | bytes 983048 | tf_op jit(solution)/shard_map/ppermute | solution.py:37
  200.3 11.1 %collective-permute-start.37 = (bf16[128,1280]{1,0:T(8,128)(2,1)S(1)}, bf16[128,1280]{1,0:T(8,128)(2,1)S(1)}, u32[]{:S(2)}, u32[]{:S(2)}) collective-permute-start(bf16[128,1280]{1,0:T(8,128)(2,1)S(1)} %get-tuple-element.74), channel_id=1, source_target_pairs={{0,18},{1,3},{2,0},{3,17},{16,2},{17,19},{18,16},{19,1},{4,22},{5,... | collective-permute-start | bytes 983048 | tf_op jit(solution)/shard_map/ppermute | solution.py:37
  200.4 13.2 %collective-permute-start.41 = (bf16[128,1280]{1,0:T(8,128)(2,1)S(1)}, bf16[128,1280]{1,0:T(8,128)(2,1)S(1)}, u32[]{:S(2)}, u32[]{:S(2)}) collective-permute-start(bf16[128,1280]{1,0:T(8,128)(2,1)S(1)} %get-tuple-element.78), channel_id=1, source_target_pairs={{0,2},{1,19},{2,16},{3,1},{16,18},{17,3},{18,0},{19,17},{4,6},{5,2... | collective-permute-start | bytes 983048 | tf_op jit(solution)/shard_map/ppermute | solution.py:37
  204.9 13.5 %collective-permute-start.35 = (bf16[128,1280]{1,0:T(8,128)(2,1)S(1)}, bf16[128,1280]{1,0:T(8,128)(2,1)S(1)}, u32[]{:S(2)}, u32[]{:S(2)}) collective-permute-start(bf16[128,1280]{1,0:T(8,128)(2,1)S(1)} %get-tuple-element.72), channel_id=1, source_target_pairs={{0,18},{1,3},{2,0},{3,17},{16,2},{17,19},{18,16},{19,1},{4,22},{5,... | collective-permute-start | bytes 983048 | tf_op jit(solution)/shard_map/ppermute | solution.py:37
  206.8 13.8 %collective-permute-start.39 = (bf16[128,1280]{1,0:T(8,128)(2,1)S(1)}, bf16[128,1280]{1,0:T(8,128)(2,1)S(1)}, u32[]{:S(2)}, u32[]{:S(2)}) collective-permute-start(bf16[128,1280]{1,0:T(8,128)(2,1)S(1)} %get-tuple-element.76), channel_id=1, source_target_pairs={{0,2},{1,19},{2,16},{3,1},{16,18},{17,3},{18,0},{19,17},{4,6},{5,2... | collective-permute-start | bytes 983048 | tf_op jit(solution)/shard_map/ppermute | solution.py:37
  209.6 15.9 %collective-permute-start.36 = (bf16[128,1280]{1,0:T(8,128)(2,1)S(1)}, bf16[128,1280]{1,0:T(8,128)(2,1)S(1)}, u32[]{:S(2)}, u32[]{:S(2)}) collective-permute-start(bf16[128,1280]{1,0:T(8,128)(2,1)S(1)} %get-tuple-element.73), channel_id=1, source_target_pairs={{0,18},{1,3},{2,0},{3,17},{16,2},{17,19},{18,16},{19,1},{4,22},{5,... | collective-permute-start | bytes 983048 | tf_op jit(solution)/shard_map/ppermute | solution.py:37
  211.4 15.7 %collective-permute-start.40 = (bf16[128,1280]{1,0:T(8,128)(2,1)S(1)}, bf16[128,1280]{1,0:T(8,128)(2,1)S(1)}, u32[]{:S(2)}, u32[]{:S(2)}) collective-permute-start(bf16[128,1280]{1,0:T(8,128)(2,1)S(1)} %get-tuple-element.77), channel_id=1, source_target_pairs={{0,2},{1,19},{2,16},{3,1},{16,18},{17,3},{18,0},{19,17},{4,6},{5,2... | collective-permute-start | bytes 983048 | tf_op jit(solution)/shard_map/ppermute | solution.py:37
  (7 other events, 16.5 us)
Sparse Core Ops, SparseCore 0:
  27.3 80.1 all-gather.1

commit v2 on v1

--- a/solution.py
+++ b/solution.py
@@ -127,12 +127,11 @@
 
 def qkv_kernel(place, *refs):
     x_refs, (b0, b1, b2a, b2b, b3) = refs[:8], refs[8:13]
-    rest_ref, live_ref, qgain_ref, kgain_ref, cos_ref, sin_ref, o_ref, w_ref, acc_ref, sems = refs[13:]
-    y, core = place[1], place[2]
+    live_ref, qgain_ref, kgain_ref, cos_ref, sin_ref, o_ref, w_ref, acc_ref, sems = refs[13:]
+    core = place[2]
     step = pl.program_id(0)
     piece = b0.shape[0] // 8
     depth = piece * 8
-    columns = b0.shape[1]
 
     def block(index, start):
         if index == 2:
@@ -165,19 +164,10 @@
     def _():
         at = pl.ds(pl.multiple_of(step * depth, 128), depth)
         pltpu.make_async_copy(w_ref.at[at], w_ref.at[at], sems.at[step]).wait()
-        rest = jnp.concatenate(
-            [
-                rest_ref[pl.ds(pl.multiple_of((h * 4 + lax.rem(e + y, 4)) * piece, 32), piece), :]
-                for h in range(2)
-                for e in range(4)
-            ],
-            axis=0,
-        )
         for g in range(2):
             x = jnp.concatenate([r[...] for r in x_refs[g * 4 : g * 4 + 4]], axis=0)
             rows = slice(g * 512, (g + 1) * 512)
-            acc_ref[rows, :columns] += jnp.dot(x, w_ref[at, :], preferred_element_type=jnp.float32)
-            acc_ref[rows, columns:] += jnp.dot(x, rest, preferred_element_type=jnp.float32)
+            acc_ref[rows, :] += jnp.dot(x, w_ref[at, :], preferred_element_type=jnp.float32)
 
     @pl.when(step >= 4)
     def _():
@@ -192,13 +182,14 @@
         )
 
 
-def qkv_attend(place, tokens, blocks, rest, row_lengths, query_gain, key_norm_gain):
+def qkv_attend(place, tokens, blocks, row_lengths, query_gain, key_norm_gain):
     sub, width = tokens[0].shape
+    tokens = [(t, part) for t in tokens for part in range(t.shape[0] // sub)]
     total = sub * len(tokens)
     head_width = query_gain.shape[0]
     slots = 32
-    heads_width = blocks[0].shape[1]
-    columns = heads_width + rest.shape[1]
+    columns = blocks[0].shape[1]
+    heads_width = columns - 2 * head_width
     depth = width // 4
     half_width = head_width // 2
     freq_index = jnp.arange(half_width, dtype=jnp.float32)
@@ -210,9 +201,6 @@
     live = (jnp.arange(slots, dtype=jnp.int32)[None, :] < row_lengths[:, None]).astype(jnp.int32)
     live = live.reshape(total // sub, 1, sub)
 
-    def rest_index(i, p):
-        return lax.rem(jnp.minimum(i, 3) + p[0], 4), 0
-
     fixed = [*blocks[:2], *blocks[2], blocks[3]]
     small = [query_gain.reshape(1, -1), key_norm_gain.reshape(1, -1), cosine, sine]
     return pl.pallas_call(
@@ -221,24 +209,23 @@
         grid_spec=pltpu.PrefetchScalarGridSpec(
             num_scalar_prefetch=1,
             grid=(12,),
-            in_specs=[pl.BlockSpec((sub, depth), lambda i, p: (0, jnp.minimum(i, 3)))] * len(tokens)
+            in_specs=[pl.BlockSpec((sub, depth), lambda i, p, part=part: (part, jnp.minimum(i, 3))) for _, part in tokens]
             + [pl.BlockSpec(memory_space=pl.ANY)] * len(fixed)
-            + [pl.BlockSpec((depth, rest.shape[1]), rest_index)]
             + [pl.BlockSpec((1, 1, sub), lambda i, p: (jnp.maximum(i, 4) - 4, 0, 0))]
             + [pl.BlockSpec(a.shape, lambda i, p: (0, 0)) for a in small],
             out_specs=pl.BlockSpec((sub, heads_width), lambda i, p: (jnp.maximum(i, 4) - 4, 0)),
             scratch_shapes=[
-                pltpu.VMEM((width, heads_width), jnp.bfloat16),
+                pltpu.VMEM((width, columns), jnp.bfloat16),
                 pltpu.VMEM((total, columns), jnp.float32),
                 pltpu.SemaphoreType.DMA((4,)),
             ],
         ),
-        compiler_params=pltpu.CompilerParams(vmem_limit_bytes=44 * MIB),
+        compiler_params=pltpu.CompilerParams(vmem_limit_bytes=46 * MIB),
         cost_estimate=pl.CostEstimate(
             flops=2 * total * width * columns, bytes_accessed=2 * (total + columns) * width, transcendentals=total * sub * 8
         ),
         name="qkv_attend",
-    )(place, *tokens, *fixed, rest, live, *small)
+    )(place, *(t for t, _ in tokens), *fixed, live, *small)
 
 
 def project(rows_ref, parts):
@@ -339,17 +326,16 @@
     rows = states.shape[0]
     piece = w_query.shape[0]
 
-    key_value = jnp.concatenate([key_weight, value_weight], axis=1)
-    rest = lax.all_gather(key_value, ("z", "xh", "y"), axis=0, tiled=True)
-
-    w_query = after(w_query, key_value)
-    w_other = shift(w_query, "xh", 1, 2)
+    weights = jnp.concatenate([w_query, key_weight, value_weight], axis=1)
+    other_weights = shift(weights, "xh", 1, 2)
     out_other = shift(w_out, "xh", 1, 2)
     other_lengths = shift(lengths, "xh", 1, 2)
     left, right = rolled_norm(states, norm_gain, place)
-    w_query, w_other, left, right = lax.optimization_barrier((w_query, w_other, left, right, other_lengths))[:4]
+    weights, other_weights, left, right = lax.optimization_barrier(
+        (weights, other_weights, left, right, other_lengths)
+    )[:4]
     w_pair = lax.dynamic_slice_in_dim(
-        jnp.concatenate([w_query, w_other, w_query], axis=0), xh * piece, 2 * piece, axis=0
+        jnp.concatenate([weights, other_weights, weights], axis=0), xh * piece, 2 * piece, axis=0
     )
 
     own = by_core(c, right, left)
@@ -370,9 +356,10 @@
     for steps in (-1, 1, 2):
         hops[-steps % 4] = shift(even, "y", steps), shift(odd, "z", steps)
         even, odd, *_ = lax.optimization_barrier((even, odd, *hops[-steps % 4]))
+    after_, before_ = lax.optimization_barrier((after_, before_))
     far = along(after_[:half], -1), along(before_[half:], 1)
     even_near, odd_near = (jnp.concatenate([hops[k][i] for k in range(4)], axis=0) for i in range(2))
-    even_near, odd_near, rest, *far = lax.optimization_barrier((even_near, odd_near, rest, *far))
+    even_near, odd_near, *far = lax.optimization_barrier((even_near, odd_near, *far))
     blocks = [near, after_, tuple(far), before_]
     up_z, down_z = shift(even_near, "z", -1), shift(even_near, "z", 1)
     up_y, down_y = shift(odd_near, "y", -1), shift(odd_near, "y", 1)
@@ -389,7 +376,7 @@
         return [*by_core(core, own[hp:], own[:hp]), *by_core(core, from_left, from_right)]
 
     row_lengths = jnp.concatenate(prompt_lengths(c) + prompt_lengths(1 - c))
-    attended = qkv_attend(place, tokens, blocks, rest, row_lengths, query_gain, key_norm_gain)
+    attended = qkv_attend(place, tokens, blocks, row_lengths, query_gain, key_norm_gain)
 
     up_z, down_z, up_y, down_y, attended = lax.optimization_barrier((up_z, down_z, up_y, down_y, attended))
     half = even_near.shape[0] // 2

time: 238 us -> 234 us (0.983)
  between operations: 13.8 us -> 0.43 us
  starting transfers between devices: 66.6 us -> 73.6 us
  local copies, waits for them, and re-layouts: 9.37 us -> 14 us
    ppermute x7, waiting for transfers between devices: 28.3 us -> 44 us  [cross_shift(): return lax.ppermute(value, ('z', 'y', 'c'), pairs)]
    ppermute x10, waiting for transfers between devices: 32.4 us -> 16.9 us  [x_shift(): return lax.ppermute(value, X + ('c',), pairs)]
    ppermute x25, starting transfers between devices: 43.2 us -> 49.4 us  [shift(): lax.ppermute(value, axis, [(i, (i + steps) % size) for i in range(size)])]
    unnamed x25 -> x40, local copies, waits for them, and re-layouts: 4.05 us -> 7.21 us
    ppermute x7, starting transfers between devices: 9.43 us -> 12.2 us  [cross_shift(): return lax.ppermute(value, ('z', 'y', 'c'), pairs)]
  transfers between devices with their start and end apart: 43 -> 42, of which waited for: 15 -> 14; matrix products, arithmetic and copies ran while one was open for 5% -> 5% of each run, Pallas kernels for 20% -> 21%
where the time goes in v2:
time: 234 us; the launch traced here: 233 us
  waiting for transfers between devices  85.6 us (37%)
  starting transfers between devices  73.6 us (31%)
  Pallas kernels  51.9 us (22%)
  local copies, waits for them, and re-layouts  14 us (6%)
  other arithmetic  7.88 us (3%)
    ppermute x25, starting transfers between devices, shift(): lax.ppermute(value, axis, [(i, (i + steps) % size) for i in range(size)])  49.4 us
    ppermute x7, waiting for transfers between devices, cross_shift(): return lax.ppermute(value, ('z', 'y', 'c'), pairs)  44 us
    pallas_call x1, Pallas kernels, qkv_attend(): pl.pallas_call(qkv_kernel, out_shape=jax.ShapeDtypeStruct((total, heads_w...  28.3 us
    ppermute x25, waiting for transfers between devices, shift(): lax.ppermute(value, axis, [(i, (i + steps) % size) for i in range(size)])  24.7 us
    ppermute x10, waiting for transfers between devices, x_shift(): return lax.ppermute(value, X + ('c',), pairs)  16.9 us
    pallas_call x8, Pallas kernels, project_call(): pl.pallas_call(functools.partial(keep_kernel if keep else give_kernel, le...  14.6 us
    ppermute x7, starting transfers between devices, cross_shift(): return lax.ppermute(value, ('z', 'y', 'c'), pairs)  12.2 us
    ppermute x10, starting transfers between devices, x_shift(): return lax.ppermute(value, X + ('c',), pairs)  12 us
  transfers between devices with their start and end apart: 42, of which 14 were waited for; matrix products, arithmetic and copies ran while one was open for 5% of the time, Pallas kernels for 21%

profile of v2, /device:TPU:1, one launch (start us, length us, event | category | flops | bytes accessed | tf_op | source)
XLA Modules:
  0.0 233.4 jit_solution(12274301352198299823)
XLA Ops:
  2.6 3.7 %collective-permute-start.1 = (bf16[160,1280]{1,0:T(8,128)(2,1)S(1)}, bf16[160,1280]{1,0:T(8,128)(2,1)S(1)}, u32[]{:S(2)}, u32[]{:S(2)}) collective-permute-start(bf16[160,1280]{1,0:T(8,128)(2,1)S(1)} %constant_dynamic-update-slice_fusion), channel_id=1, source_target_pairs={{0,16},{16,0},{1,17},{17,1},{2,18},{18,2},{3,19},{19,3},{4,20},{20... | collective-permute-start | bytes 1228808 | tf_op jit(solution)/shard_map/ppermute | solution.py:18
  6.4 1.7 copy-done.1
  8.9 5.2 %norm.1 = (bf16[128,5120]{1,0:T(8,128)(2,1)S(1)}, bf16[128,5120]{1,0:T(8,128)(2,1)S(1)}) custom-call(s32[3]{0:T(128)S(1)} %pad_add_fusion.place, bf16[256,5120]{1,0:T(8,128)(2,1)S(1)} %copy-done.1, f32[1,5120]{1,0:T(1,128)S(1)} %bitcast.10), custom_call_target="tpu_custom_call" | custom-call | flops 7864320 | bytes 5242880 | tf_op jit(solution)/shard_map/norm/pallas_call | solution.py:73
  17.3 1.8 collective-permute-start.5
  19.1 3.3 %collective-permute-start.4 = (bf16[320,1280]{1,0:T(8,128)(2,1)S(1)}, bf16[320,1280]{1,0:T(8,128)(2,1)S(1)}, u32[]{:S(2)}, u32[]{:S(2)}) collective-permute-start(bf16[320,1280]{1,0:T(8,128)(2,1)S(1)} %fusion.1), channel_id=1, source_target_pairs={{0,8},{1,65},{4,12},{5,69},{8,0},{9,73},{12,4},{13,77},{32,40},{33... | collective-permute-start | bytes 2457608 | tf_op jit(solution)/shard_map/ppermute | solution.py:29
  23.2 8.1 %collective-permute-done.5 = bf16[320,1280]{1,0:T(8,128)(2,1)S(1)} collective-permute-done((bf16[320,1280]{1,0:T(8,128)(2,1)S(1)}, bf16[320,1280]{1,0:T(8,128)(2,1)S(1)}, u32[]{:S(2)}, u32[]{:S(2)}) %collective-permute-start.5) | collective-permute-done | bytes 819232 | tf_op jit(solution)/shard_map/ppermute | solution.py:29
  31.3 10.0 %collective-permute-done.4 = bf16[320,1280]{1,0:T(8,128)(2,1)S(1)} collective-permute-done((bf16[320,1280]{1,0:T(8,128)(2,1)S(1)}, bf16[320,1280]{1,0:T(8,128)(2,1)S(1)}, u32[]{:S(2)}, u32[]{:S(2)}) %collective-permute-start.4) | collective-permute-done | bytes 819232 | tf_op jit(solution)/shard_map/ppermute | solution.py:29
  41.2 1.9 pad_maximum_fusion.refs_8_
  45.8 2.7 %collective-permute-start = (bf16[160,1024]{1,0:T(8,128)(2,1)S(1)}, bf16[160,1024]{1,0:T(8,128)(2,1)S(1)}, u32[]{:S(2)}, u32[]{:S(2)}) collective-permute-start(bf16[160,1024]{1,0:T(8,128)(2,1)S(1)} %copy-done.16), channel_id=1, source_target_pairs={{0,16},{16,0},{1,17},{17,1},{2,18},{18,2},{3,19},{19,3},{4,20},{20... | collective-permute-start | bytes 983048 | tf_op jit(solution)/shard_map/ppermute | solution.py:18
  48.5 1.9 broadcast_select_fusion
  50.4 3.6 %collective-permute-done = bf16[160,1024]{1,0:T(8,128)(2,1)S(1)} collective-permute-done((bf16[160,1024]{1,0:T(8,128)(2,1)S(1)}, bf16[160,1024]{1,0:T(8,128)(2,1)S(1)}, u32[]{:S(2)}, u32[]{:S(2)}) %collective-permute-start) | collective-permute-done | bytes 327712 | tf_op jit(solution)/shard_map/ppermute | solution.py:18
  54.1 2.5 %collective-permute-start.20 = (bf16[128,5120]{1,0:T(8,128)(2,1)S(1)}, bf16[128,5120]{1,0:T(8,128)(2,1)}, u32[]{:S(2)}, u32[]{:S(2)}) collective-permute-start(bf16[128,5120]{1,0:T(8,128)(2,1)S(1)} %get-tuple-element.58.refs_0_), channel_id=1, source_target_pairs={{0,2},{1,19},{2,16},{3,1},{16,18},{17,3},{18,0},{19,17},{4,6},{5,2... | collective-permute-start | bytes 3932168 | tf_op jit(solution)/shard_map/ppermute | solution.py:37
  56.6 25.9 %collective-permute-done.13.refs_12_ = bf16[1280,1280]{1,0:T(8,128)(2,1)} collective-permute-done((bf16[1280,1280]{1,0:T(8,128)(2,1)}, bf16[1280,1280]{1,0:T(8,128)(2,1)}, u32[]{:S(2)}, u32[]{:S(2)}) %collective-permute-start.13) | collective-permute-done | bytes 3276832 | tf_op jit(solution)/shard_map/ppermute | solution.py:29
  82.5 2.7 %slice.43 = bf16[640,1280]{1,0:T(8,128)(2,1)} slice(bf16[1280,1280]{1,0:T(8,128)(2,1)} %collective-permute-done.13.refs_12_), slice={[640:1280], [0:1280]} | slice | bytes 3276800 | tf_op jit(solution)/shard_map/slice | solution.py:360
  88.6 1.7 collective-permute-start.6
  90.3 1.9 collective-permute-start.7
  92.3 2.7 %collective-permute-done.6 = bf16[160,1024]{1,0:T(8,128)(2,1)S(1)} collective-permute-done((bf16[160,1024]{1,0:T(8,128)(2,1)S(1)}, bf16[160,1024]{1,0:T(8,128)(2,1)S(1)}, u32[]{:S(2)}, u32[]{:S(2)}) %collective-permute-start.6) | collective-permute-done | bytes 327712 | tf_op jit(solution)/shard_map/ppermute | solution.py:18
  98.5 2.7 %slice.42 = bf16[640,1280]{1,0:T(8,128)(2,1)} slice(bf16[1280,1280]{1,0:T(8,128)(2,1)} %collective-permute-done.12.refs_9_), slice={[0:640], [0:1280]} | slice | bytes 3276800 | tf_op jit(solution)/shard_map/slice | solution.py:360
  101.2 2.6 %collective-permute-start.14 = (bf16[640,1280]{1,0:T(8,128)(2,1)}, bf16[640,1280]{1,0:T(8,128)(2,1)}, u32[]{:S(2)}, u32[]{:S(2)}) collective-permute-start(bf16[640,1280]{1,0:T(8,128)(2,1)} %slice.42), channel_id=1, source_target_pairs={{0,96},{1,13},{4,100},{5,1},{8,104},{9,5},{12,108},{13,9},{32,0},{... | collective-permute-start | bytes 4915208 | tf_op jit(solution)/shard_map/ppermute | solution.py:29
  103.7 8.9 %collective-permute-done.8 = bf16[160,1024]{1,0:T(8,128)(2,1)S(1)} collective-permute-done((bf16[160,1024]{1,0:T(8,128)(2,1)S(1)}, bf16[160,1024]{1,0:T(8,128)(2,1)S(1)}, u32[]{:S(2)}, u32[]{:S(2)}) %collective-permute-start.8) | collective-permute-done | bytes 327712 | tf_op jit(solution)/shard_map/ppermute | solution.py:18
  112.6 2.5 %collective-permute-start.10 = (bf16[160,1024]{1,0:T(8,128)(2,1)S(1)}, bf16[160,1024]{1,0:T(8,128)(2,1)S(1)}, u32[]{:S(2)}, u32[]{:S(2)}) collective-permute-start(bf16[160,1024]{1,0:T(8,128)(2,1)S(1)} %get-tuple-element.50), channel_id=1, source_target_pairs={{0,8},{4,12},{8,0},{12,4},{1,9},{5,13},{9,1},{13,5},{2,10},{6,14},... | collective-permute-start | bytes 983048 | tf_op jit(solution)/shard_map/ppermute | solution.py:18
  115.1 1.9 collective-permute-start.11
  117.0 3.1 %collective-permute-done.10 = bf16[160,1024]{1,0:T(8,128)(2,1)S(1)} collective-permute-done((bf16[160,1024]{1,0:T(8,128)(2,1)S(1)}, bf16[160,1024]{1,0:T(8,128)(2,1)S(1)}, u32[]{:S(2)}, u32[]{:S(2)}) %collective-permute-start.10) | collective-permute-done | bytes 327712 | tf_op jit(solution)/shard_map/ppermute | solution.py:18
  120.1 6.0 %collective-permute-start.23 = (bf16[128,5120]{1,0:T(8,128)(2,1)S(1)}, bf16[128,5120]{1,0:T(8,128)(2,1)}, u32[]{:S(2)}, u32[]{:S(2)}) collective-permute-start(bf16[128,5120]{1,0:T(8,128)(2,1)S(1)} %get-tuple-element.59.refs_1_), channel_id=1, source_target_pairs={{0,1},{1,0},{2,3},{3,2},{4,5},{5,4},{6,7},{7,6},{8,9},{9,8},{10,11... | collective-permute-start | bytes 3932168 | tf_op jit(solution)/shard_map/ppermute | solution.py:18
  126.1 5.0 %collective-permute-start.22 = (bf16[128,5120]{1,0:T(8,128)(2,1)S(1)}, bf16[128,5120]{1,0:T(8,128)(2,1)}, u32[]{:S(2)}, u32[]{:S(2)}) collective-permute-start(bf16[128,5120]{1,0:T(8,128)(2,1)S(1)} %get-tuple-element.58.refs_0_), channel_id=1, source_target_pairs={{0,1},{1,0},{2,3},{3,2},{4,5},{5,4},{6,7},{7,6},{8,9},{9,8},{10,11... | collective-permute-start | bytes 3932168 | tf_op jit(solution)/shard_map/ppermute | solution.py:18
  134.4 7.0 %collective-permute-start.17 = (bf16[640,1024]{1,0:T(8,128)(2,1)S(1)}, bf16[640,1024]{1,0:T(8,128)(2,1)S(1)}, u32[]{:S(2)}, u32[]{:S(2)}) collective-permute-start(bf16[640,1024]{1,0:T(8,128)(2,1)S(1)} %pad_maximum_fusion.1.refs_0_), channel_id=1, source_target_pairs={{0,32},{32,64},{64,96},{96,0},{1,33},{33,65},{65,97},{97,1},{2,34}... | collective-permute-start | bytes 3932168 | tf_op jit(solution)/shard_map/ppermute | solution.py:18
  143.5 2.1 collective-permute-start.18
  145.7 28.3 %qkv_attend.1.rows_ref = bf16[1024,1024]{1,0:T(8,128)(2,1)} custom-call(s32[3]{0:T(128)S(1)} %pad_add_fusion.place, bf16[128,5120]{1,0:T(8,128)(2,1)S(1)} %get-tuple-element.58.refs_0_, bf16[128,5120]{1,0:T(8,128)(2,1)S(1)} %get-tuple-element.59.refs_1_, bf16[128,5120]{1,0:T(8,128)(2,1)} %collective-permute-done.20.refs_2_, ...), custom_call_target="tpu_custom_call" | custom-call | flops 13421772800 | bytes 23592960 | tf_op jit(solution)/shard_map/qkv_attend/pallas_call | solution.py:206
  174.9 2.7 %collective-permute-start.30 = (bf16[320,1024]{1,0:T(8,128)(2,1)S(1)}, bf16[320,1024]{1,0:T(8,128)(2,1)S(1)}, u32[]{:S(2)}, u32[]{:S(2)}) collective-permute-start(bf16[320,1024]{1,0:T(8,128)(2,1)S(1)} %slice.54), channel_id=1, source_target_pairs={{0,12},{4,0},{8,4},{12,8},{1,13},{5,1},{9,5},{13,9},{2,14},{6,2},{... | collective-permute-start | bytes 1966088 | tf_op jit(solution)/shard_map/ppermute | solution.py:18
  177.6 2.1 collective-permute-start.28
  179.8 1.8 give.4
  181.6 2.3 collective-permute-start.26
  183.9 1.8 give.7
  185.7 4.7 %collective-permute-done.31.refs_3_ = bf16[320,1024]{1,0:T(8,128)(2,1)S(1)} collective-permute-done((bf16[320,1024]{1,0:T(8,128)(2,1)S(1)}, bf16[320,1024]{1,0:T(8,128)(2,1)S(1)}, u32[]{:S(2)}, u32[]{:S(2)}) %collective-permute-start.31) | collective-permute-done | bytes 655392 | tf_op jit(solution)/shard_map/ppermute | solution.py:18
  190.4 2.0 collective-permute-start.33
  192.5 1.8 give.5
  194.6 1.8 give.6
  197.0 1.8 keep.4
  199.0 2.7 %collective-permute-start.38 = (bf16[128,1280]{1,0:T(8,128)(2,1)S(1)}, bf16[128,1280]{1,0:T(8,128)(2,1)S(1)}, u32[]{:S(2)}, u32[]{:S(2)}) collective-permute-start(bf16[128,1280]{1,0:T(8,128)(2,1)S(1)} %get-tuple-element.75), channel_id=1, source_target_pairs={{0,2},{1,19},{2,16},{3,1},{16,18},{17,3},{18,0},{19,17},{4,6},{5,2... | collective-permute-start | bytes 983048 | tf_op jit(solution)/shard_map/ppermute | solution.py:37
  201.6 1.8 keep.7
  203.6 2.7 %collective-permute-start.41 = (bf16[128,1280]{1,0:T(8,128)(2,1)S(1)}, bf16[128,1280]{1,0:T(8,128)(2,1)S(1)}, u32[]{:S(2)}, u32[]{:S(2)}) collective-permute-start(bf16[128,1280]{1,0:T(8,128)(2,1)S(1)} %get-tuple-element.78), channel_id=1, source_target_pairs={{0,2},{1,19},{2,16},{3,1},{16,18},{17,3},{18,0},{19,17},{4,6},{5,2... | collective-permute-start | bytes 983048 | tf_op jit(solution)/shard_map/ppermute | solution.py:37
  206.2 1.8 keep.5
  208.2 1.8 keep.6
  210.0 2.7 %collective-permute-start.39 = (bf16[128,1280]{1,0:T(8,128)(2,1)S(1)}, bf16[128,1280]{1,0:T(8,128)(2,1)S(1)}, u32[]{:S(2)}, u32[]{:S(2)}) collective-permute-start(bf16[128,1280]{1,0:T(8,128)(2,1)S(1)} %get-tuple-element.76), channel_id=1, source_target_pairs={{0,2},{1,19},{2,16},{3,1},{16,18},{17,3},{18,0},{19,17},{4,6},{5,2... | collective-permute-start | bytes 983048 | tf_op jit(solution)/shard_map/ppermute | solution.py:37
  212.7 2.8 %collective-permute-done.37.refs_7_ = bf16[128,1280]{1,0:T(8,128)(2,1)S(1)} collective-permute-done((bf16[128,1280]{1,0:T(8,128)(2,1)S(1)}, bf16[128,1280]{1,0:T(8,128)(2,1)S(1)}, u32[]{:S(2)}, u32[]{:S(2)}) %collective-permute-start.37) | collective-permute-done | bytes 327712 | tf_op jit(solution)/shard_map/ppermute | solution.py:37
  216.2 6.3 %collective-permute-done.35.refs_5_ = bf16[128,1280]{1,0:T(8,128)(2,1)S(1)} collective-permute-done((bf16[128,1280]{1,0:T(8,128)(2,1)S(1)}, bf16[128,1280]{1,0:T(8,128)(2,1)S(1)}, u32[]{:S(2)}, u32[]{:S(2)}) %collective-permute-start.35) | collective-permute-done | bytes 327712 | tf_op jit(solution)/shard_map/ppermute | solution.py:37
  223.3 6.3 %collective-permute-done.36.refs_6_ = bf16[128,1280]{1,0:T(8,128)(2,1)S(1)} collective-permute-done((bf16[128,1280]{1,0:T(8,128)(2,1)S(1)}, bf16[128,1280]{1,0:T(8,128)(2,1)S(1)}, u32[]{:S(2)}, u32[]{:S(2)}) %collective-permute-start.36) | collective-permute-done | bytes 327712 | tf_op jit(solution)/shard_map/ppermute | solution.py:37
  229.6 3.8 %finish.1 = bf16[256,5120]{1,0:T(8,128)(2,1)} custom-call(s32[3]{0:T(128)S(1)} %pad_add_fusion.place, f32[256,1280]{1,0:T(8,128)S(1)} %get-tuple-element.63.refs_0_, f32[256,1280]{1,0:T(8,128)S(1)} %get-tuple-element.66.refs_1_, f32[256,1280]{1,0:T(8,128)S(1)} %get-tuple-element.69.refs_2_, f32[256,1280]{1,0:T(8,128)S(1)} %get-tuple-element.70.refs_3_, ...), custom_call_target="tpu_custom_call" | custom-call | flops 2621440 | bytes 10485760 | tf_op jit(solution)/shard_map/finish/pallas_call | solution.py:305
  (116 shorter events, 25.6 us)
Async XLA Ops:
  2.6 13.7 %collective-permute-start.1 = (bf16[160,1280]{1,0:T(8,128)(2,1)S(1)}, bf16[160,1280]{1,0:T(8,128)(2,1)S(1)}, u32[]{:S(2)}, u32[]{:S(2)}) collective-permute-start(bf16[160,1280]{1,0:T(8,128)(2,1)S(1)} %constant_dynamic-update-slice_fusion), channel_id=1, source_target_pairs={{0,16},{16,0},{1,17},{17,1},{2,18},{18,2},{3,19},{19,3},{4,20},{20... | collective-permute-start | bytes 1228808 | tf_op jit(solution)/shard_map/ppermute | solution.py:18
  6.2 10.0 %collective-permute-start.2 = (s32[32]{0:T(128)}, s32[32]{0:T(128)S(1)}, u32[]{:S(2)}, u32[]{:S(2)}) collective-permute-start(s32[32]{0:T(128)} %param.13), channel_id=1, source_target_pairs={{0,16},{16,0},{1,17},{17,1},{2,18},{18,2},{3,19},{19,3},{4,20},{20... | collective-permute-start | bytes 392 | tf_op jit(solution)/shard_map/ppermute | solution.py:18
  17.3 28.5 %copy-start.16 = (bf16[160,1024]{1,0:T(8,128)(2,1)S(1)}, bf16[160,1024]{1,0:T(8,128)(2,1)}, u32[]{:S(2)}) copy-start(bf16[160,1024]{1,0:T(8,128)(2,1)} %param.17) | copy-start | bytes 983044
  17.3 14.0 %collective-permute-start.5 = (bf16[320,1280]{1,0:T(8,128)(2,1)S(1)}, bf16[320,1280]{1,0:T(8,128)(2,1)S(1)}, u32[]{:S(2)}, u32[]{:S(2)}) collective-permute-start(bf16[320,1280]{1,0:T(8,128)(2,1)S(1)} %fusion.1), channel_id=1, source_target_pairs={{0,4},{1,33},{4,8},{5,37},{8,12},{9,41},{12,0},{13,45},{32,36},{33... | collective-permute-start | bytes 2457608 | tf_op jit(solution)/shard_map/ppermute | solution.py:29
  19.1 22.1 %collective-permute-start.4 = (bf16[320,1280]{1,0:T(8,128)(2,1)S(1)}, bf16[320,1280]{1,0:T(8,128)(2,1)S(1)}, u32[]{:S(2)}, u32[]{:S(2)}) collective-permute-start(bf16[320,1280]{1,0:T(8,128)(2,1)S(1)} %fusion.1), channel_id=1, source_target_pairs={{0,8},{1,65},{4,12},{5,69},{8,0},{9,73},{12,4},{13,77},{32,40},{33... | collective-permute-start | bytes 2457608 | tf_op jit(solution)/shard_map/ppermute | solution.py:29
  22.4 18.8 %collective-permute-start.3 = (bf16[320,1280]{1,0:T(8,128)(2,1)S(1)}, bf16[320,1280]{1,0:T(8,128)(2,1)S(1)}, u32[]{:S(2)}, u32[]{:S(2)}) collective-permute-start(bf16[320,1280]{1,0:T(8,128)(2,1)S(1)} %fusion.1), channel_id=1, source_target_pairs={{0,12},{1,97},{4,0},{5,101},{8,4},{9,105},{12,8},{13,109},{32,44},... | collective-permute-start | bytes 2457608 | tf_op jit(solution)/shard_map/ppermute | solution.py:29
  43.1 39.3 %collective-permute-start.13 = (bf16[1280,1280]{1,0:T(8,128)(2,1)}, bf16[1280,1280]{1,0:T(8,128)(2,1)}, u32[]{:S(2)}, u32[]{:S(2)}) collective-permute-start(bf16[1280,1280]{1,0:T(8,128)(2,1)} %pad_maximum_fusion.refs_8_), channel_id=1, source_target_pairs={{0,32},{1,5},{4,36},{5,9},{8,40},{9,13},{12,44},{13,1},{32,64},{33... | collective-permute-start | bytes 9830408 | tf_op jit(solution)/shard_map/ppermute | solution.py:29
  44.1 38.3 %collective-permute-start.12 = (bf16[1280,1280]{1,0:T(8,128)(2,1)}, bf16[1280,1280]{1,0:T(8,128)(2,1)}, u32[]{:S(2)}, u32[]{:S(2)}) collective-permute-start(bf16[1280,1280]{1,0:T(8,128)(2,1)} %pad_maximum_fusion.refs_8_), channel_id=1, source_target_pairs={{0,96},{1,13},{4,100},{5,1},{8,104},{9,5},{12,108},{13,9},{32,0},{... | collective-permute-start | bytes 9830408 | tf_op jit(solution)/shard_map/ppermute | solution.py:29
  45.8 8.3 %collective-permute-start = (bf16[160,1024]{1,0:T(8,128)(2,1)S(1)}, bf16[160,1024]{1,0:T(8,128)(2,1)S(1)}, u32[]{:S(2)}, u32[]{:S(2)}) collective-permute-start(bf16[160,1024]{1,0:T(8,128)(2,1)S(1)} %copy-done.16), channel_id=1, source_target_pairs={{0,16},{16,0},{1,17},{17,1},{2,18},{18,2},{3,19},{19,3},{4,20},{20... | collective-permute-start | bytes 983048 | tf_op jit(solution)/shard_map/ppermute | solution.py:18
  54.1 31.1 %copy-start.17 = (bf16[160,1024]{1,0:T(8,128)(2,1)}, bf16[160,1024]{1,0:T(8,128)(2,1)S(1)}, u32[]{:S(2)}) copy-start(bf16[160,1024]{1,0:T(8,128)(2,1)S(1)} %collective-permute-done) | copy-start | bytes 983044
  54.1 32.2 %collective-permute-start.20 = (bf16[128,5120]{1,0:T(8,128)(2,1)S(1)}, bf16[128,5120]{1,0:T(8,128)(2,1)}, u32[]{:S(2)}, u32[]{:S(2)}) collective-permute-start(bf16[128,5120]{1,0:T(8,128)(2,1)S(1)} %get-tuple-element.58.refs_0_), channel_id=1, source_target_pairs={{0,2},{1,19},{2,16},{3,1},{16,18},{17,3},{18,0},{19,17},{4,6},{5,2... | collective-permute-start | bytes 3932168 | tf_op jit(solution)/shard_map/ppermute | solution.py:37
  85.2 46.8 %collective-permute-start.15 = (bf16[640,1280]{1,0:T(8,128)(2,1)}, bf16[640,1280]{1,0:T(8,128)(2,1)}, u32[]{:S(2)}, u32[]{:S(2)}) collective-permute-start(bf16[640,1280]{1,0:T(8,128)(2,1)} %slice.43), channel_id=1, source_target_pairs={{0,32},{1,5},{4,36},{5,9},{8,40},{9,13},{12,44},{13,1},{32,64},{33... | collective-permute-start | bytes 4915208 | tf_op jit(solution)/shard_map/ppermute | solution.py:29
  86.3 44.9 %collective-permute-start.21 = (bf16[128,5120]{1,0:T(8,128)(2,1)S(1)}, bf16[128,5120]{1,0:T(8,128)(2,1)}, u32[]{:S(2)}, u32[]{:S(2)}) collective-permute-start(bf16[128,5120]{1,0:T(8,128)(2,1)S(1)} %get-tuple-element.59.refs_1_), channel_id=1, source_target_pairs={{0,18},{1,3},{2,0},{3,17},{16,2},{17,19},{18,16},{19,1},{4,22},{5,... | collective-permute-start | bytes 3932168 | tf_op jit(solution)/shard_map/ppermute | solution.py:37
  88.6 43.7 %copy-start.18 = (s32[32]{0:T(128)S(1)}, s32[32]{0:T(128)}, u32[]{:S(2)}) copy-start(s32[32]{0:T(128)} %param.13) | copy-start | bytes 388
  88.6 6.4 %collective-permute-start.6 = (bf16[160,1024]{1,0:T(8,128)(2,1)S(1)}, bf16[160,1024]{1,0:T(8,128)(2,1)S(1)}, u32[]{:S(2)}, u32[]{:S(2)}) collective-permute-start(bf16[160,1024]{1,0:T(8,128)(2,1)S(1)} %get-tuple-element.50), channel_id=1, source_target_pairs={{0,12},{4,0},{8,4},{12,8},{1,13},{5,1},{9,5},{13,9},{2,14},{6,2},{... | collective-permute-start | bytes 983048 | tf_op jit(solution)/shard_map/ppermute | solution.py:18
  90.3 6.3 %collective-permute-start.7 = (bf16[160,1024]{1,0:T(8,128)(2,1)S(1)}, bf16[160,1024]{1,0:T(8,128)(2,1)S(1)}, u32[]{:S(2)}, u32[]{:S(2)}) collective-permute-start(bf16[160,1024]{1,0:T(8,128)(2,1)S(1)} %get-tuple-element.51), channel_id=1, source_target_pairs={{0,96},{32,0},{64,32},{96,64},{1,97},{33,1},{65,33},{97,65},{2,98}... | collective-permute-start | bytes 983048 | tf_op jit(solution)/shard_map/ppermute | solution.py:18
  97.4 15.2 %collective-permute-start.8 = (bf16[160,1024]{1,0:T(8,128)(2,1)S(1)}, bf16[160,1024]{1,0:T(8,128)(2,1)S(1)}, u32[]{:S(2)}, u32[]{:S(2)}) collective-permute-start(bf16[160,1024]{1,0:T(8,128)(2,1)S(1)} %get-tuple-element.50), channel_id=1, source_target_pairs={{0,4},{4,8},{8,12},{12,0},{1,5},{5,9},{9,13},{13,1},{2,6},{6,10},{... | collective-permute-start | bytes 983048 | tf_op jit(solution)/shard_map/ppermute | solution.py:18
  97.4 15.2 %collective-permute-start.9 = (bf16[160,1024]{1,0:T(8,128)(2,1)S(1)}, bf16[160,1024]{1,0:T(8,128)(2,1)S(1)}, u32[]{:S(2)}, u32[]{:S(2)}) collective-permute-start(bf16[160,1024]{1,0:T(8,128)(2,1)S(1)} %get-tuple-element.51), channel_id=1, source_target_pairs={{0,32},{32,64},{64,96},{96,0},{1,33},{33,65},{65,97},{97,1},{2,34}... | collective-permute-start | bytes 983048 | tf_op jit(solution)/shard_map/ppermute | solution.py:18
  101.2 33.2 %collective-permute-start.14 = (bf16[640,1280]{1,0:T(8,128)(2,1)}, bf16[640,1280]{1,0:T(8,128)(2,1)}, u32[]{:S(2)}, u32[]{:S(2)}) collective-permute-start(bf16[640,1280]{1,0:T(8,128)(2,1)} %slice.42), channel_id=1, source_target_pairs={{0,96},{1,13},{4,100},{5,1},{8,104},{9,5},{12,108},{13,9},{32,0},{... | collective-permute-start | bytes 4915208 | tf_op jit(solution)/shard_map/ppermute | solution.py:29
  112.6 18.6 %copy-start.12 = (bf16[160,1024]{1,0:T(8,128)(2,1)}, bf16[160,1024]{1,0:T(8,128)(2,1)S(1)}, u32[]{:S(2)}) copy-start(bf16[160,1024]{1,0:T(8,128)(2,1)S(1)} %collective-permute-done.8) | copy-start | bytes 983044
  112.6 18.5 %copy-start.10 = (bf16[160,1024]{1,0:T(8,128)(2,1)}, bf16[160,1024]{1,0:T(8,128)(2,1)S(1)}, u32[]{:S(2)}) copy-start(bf16[160,1024]{1,0:T(8,128)(2,1)S(1)} %collective-permute-done.9) | copy-start | bytes 983044
  112.6 7.5 %collective-permute-start.10 = (bf16[160,1024]{1,0:T(8,128)(2,1)S(1)}, bf16[160,1024]{1,0:T(8,128)(2,1)S(1)}, u32[]{:S(2)}, u32[]{:S(2)}) collective-permute-start(bf16[160,1024]{1,0:T(8,128)(2,1)S(1)} %get-tuple-element.50), channel_id=1, source_target_pairs={{0,8},{4,12},{8,0},{12,4},{1,9},{5,13},{9,1},{13,5},{2,10},{6,14},... | collective-permute-start | bytes 983048 | tf_op jit(solution)/shard_map/ppermute | solution.py:18
  115.1 11.0 %collective-permute-start.11 = (bf16[160,1024]{1,0:T(8,128)(2,1)S(1)}, bf16[160,1024]{1,0:T(8,128)(2,1)S(1)}, u32[]{:S(2)}, u32[]{:S(2)}) collective-permute-start(bf16[160,1024]{1,0:T(8,128)(2,1)S(1)} %get-tuple-element.51), channel_id=1, source_target_pairs={{0,64},{32,96},{64,0},{96,32},{1,65},{33,97},{65,1},{97,33},{2,66}... | collective-permute-start | bytes 983048 | tf_op jit(solution)/shard_map/ppermute | solution.py:18
  120.1 21.3 %collective-permute-start.23 = (bf16[128,5120]{1,0:T(8,128)(2,1)S(1)}, bf16[128,5120]{1,0:T(8,128)(2,1)}, u32[]{:S(2)}, u32[]{:S(2)}) collective-permute-start(bf16[128,5120]{1,0:T(8,128)(2,1)S(1)} %get-tuple-element.59.refs_1_), channel_id=1, source_target_pairs={{0,1},{1,0},{2,3},{3,2},{4,5},{5,4},{6,7},{7,6},{8,9},{9,8},{10,11... | collective-permute-start | bytes 3932168 | tf_op jit(solution)/shard_map/ppermute | solution.py:18
  126.1 16.3 %collective-permute-start.22 = (bf16[128,5120]{1,0:T(8,128)(2,1)S(1)}, bf16[128,5120]{1,0:T(8,128)(2,1)}, u32[]{:S(2)}, u32[]{:S(2)}) collective-permute-start(bf16[128,5120]{1,0:T(8,128)(2,1)S(1)} %get-tuple-element.58.refs_0_), channel_id=1, source_target_pairs={{0,1},{1,0},{2,3},{3,2},{4,5},{5,4},{6,7},{7,6},{8,9},{9,8},{10,11... | collective-permute-start | bytes 3932168 | tf_op jit(solution)/shard_map/ppermute | solution.py:18
  131.2 12.3 %collective-permute-start.24 = (bf16[128,5120]{1,0:T(8,128)(2,1)}, bf16[128,5120]{1,0:T(8,128)(2,1)}, u32[]{:S(2)}, u32[]{:S(2)}) collective-permute-start(bf16[128,5120]{1,0:T(8,128)(2,1)} %collective-permute-done.20.refs_2_), channel_id=1, source_target_pairs={{0,1},{1,0},{2,3},{3,2},{4,5},{5,4},{6,7},{7,6},{8,9},{9,8},{10,11... | collective-permute-start | bytes 3932168 | tf_op jit(solution)/shard_map/ppermute | solution.py:18
  132.0 13.6 %collective-permute-start.25 = (bf16[128,5120]{1,0:T(8,128)(2,1)}, bf16[128,5120]{1,0:T(8,128)(2,1)}, u32[]{:S(2)}, u32[]{:S(2)}) collective-permute-start(bf16[128,5120]{1,0:T(8,128)(2,1)} %collective-permute-done.21.refs_3_), channel_id=1, source_target_pairs={{0,1},{1,0},{2,3},{3,2},{4,5},{5,4},{6,7},{7,6},{8,9},{9,8},{10,11... | collective-permute-start | bytes 3932168 | tf_op jit(solution)/shard_map/ppermute | solution.py:18
  134.3 11.4 %copy-start.6 = (f32[128]{0:T(128)S(1)}, f32[128]{0:T(128)}, u32[]{:S(2)}) copy-start(f32[128]{0:T(128)} %param.12) | copy-start | bytes 1540
  134.4 39.5 %collective-permute-start.17 = (bf16[640,1024]{1,0:T(8,128)(2,1)S(1)}, bf16[640,1024]{1,0:T(8,128)(2,1)S(1)}, u32[]{:S(2)}, u32[]{:S(2)}) collective-permute-start(bf16[640,1024]{1,0:T(8,128)(2,1)S(1)} %pad_maximum_fusion.1.refs_0_), channel_id=1, source_target_pairs={{0,32},{32,64},{64,96},{96,0},{1,33},{33,65},{65,97},{97,1},{2,34}... | collective-permute-start | bytes 3932168 | tf_op jit(solution)/shard_map/ppermute | solution.py:18
  141.4 32.5 %collective-permute-start.16 = (bf16[640,1024]{1,0:T(8,128)(2,1)S(1)}, bf16[640,1024]{1,0:T(8,128)(2,1)S(1)}, u32[]{:S(2)}, u32[]{:S(2)}) collective-permute-start(bf16[640,1024]{1,0:T(8,128)(2,1)S(1)} %pad_maximum_fusion.1.refs_0_), channel_id=1, source_target_pairs={{0,96},{32,0},{64,32},{96,64},{1,97},{33,1},{65,33},{97,65},{2,98}... | collective-permute-start | bytes 3932168 | tf_op jit(solution)/shard_map/ppermute | solution.py:18
  142.4 31.6 %collective-permute-start.19 = (bf16[640,1024]{1,0:T(8,128)(2,1)S(1)}, bf16[640,1024]{1,0:T(8,128)(2,1)S(1)}, u32[]{:S(2)}, u32[]{:S(2)}) collective-permute-start(bf16[640,1024]{1,0:T(8,128)(2,1)S(1)} %pad_maximum_fusion.2.refs_1_), channel_id=1, source_target_pairs={{0,4},{4,8},{8,12},{12,0},{1,5},{5,9},{9,13},{13,1},{2,6},{6,10},{... | collective-permute-start | bytes 3932168 | tf_op jit(solution)/shard_map/ppermute | solution.py:18
  143.5 30.5 %collective-permute-start.18 = (bf16[640,1024]{1,0:T(8,128)(2,1)S(1)}, bf16[640,1024]{1,0:T(8,128)(2,1)S(1)}, u32[]{:S(2)}, u32[]{:S(2)}) collective-permute-start(bf16[640,1024]{1,0:T(8,128)(2,1)S(1)} %pad_maximum_fusion.2.refs_1_), channel_id=1, source_target_pairs={{0,12},{4,0},{8,4},{12,8},{1,13},{5,1},{9,5},{13,9},{2,14},{6,2},{... | collective-permute-start | bytes 3932168 | tf_op jit(solution)/shard_map/ppermute | solution.py:18
  174.0 16.4 %collective-permute-start.31 = (bf16[320,1024]{1,0:T(8,128)(2,1)S(1)}, bf16[320,1024]{1,0:T(8,128)(2,1)S(1)}, u32[]{:S(2)}, u32[]{:S(2)}) collective-permute-start(bf16[320,1024]{1,0:T(8,128)(2,1)S(1)} %slice.55), channel_id=1, source_target_pairs={{0,4},{4,8},{8,12},{12,0},{1,5},{5,9},{9,13},{13,1},{2,6},{6,10},{... | collective-permute-start | bytes 1966088 | tf_op jit(solution)/shard_map/ppermute | solution.py:18
  174.5 19.8 %collective-permute-start.29 = (bf16[320,1024]{1,0:T(8,128)(2,1)S(1)}, bf16[320,1024]{1,0:T(8,128)(2,1)S(1)}, u32[]{:S(2)}, u32[]{:S(2)}) collective-permute-start(bf16[320,1024]{1,0:T(8,128)(2,1)S(1)} %slice.53), channel_id=1, source_target_pairs={{0,32},{32,64},{64,96},{96,0},{1,33},{33,65},{65,97},{97,1},{2,34}... | collective-permute-start | bytes 1966088 | tf_op jit(solution)/shard_map/ppermute | solution.py:18
  174.9 19.7 %collective-permute-start.30 = (bf16[320,1024]{1,0:T(8,128)(2,1)S(1)}, bf16[320,1024]{1,0:T(8,128)(2,1)S(1)}, u32[]{:S(2)}, u32[]{:S(2)}) collective-permute-start(bf16[320,1024]{1,0:T(8,128)(2,1)S(1)} %slice.54), channel_id=1, source_target_pairs={{0,12},{4,0},{8,4},{12,8},{1,13},{5,1},{9,5},{13,9},{2,14},{6,2},{... | collective-permute-start | bytes 1966088 | tf_op jit(solution)/shard_map/ppermute | solution.py:18
  177.6 17.0 %collective-permute-start.28 = (bf16[320,1024]{1,0:T(8,128)(2,1)S(1)}, bf16[320,1024]{1,0:T(8,128)(2,1)S(1)}, u32[]{:S(2)}, u32[]{:S(2)}) collective-permute-start(bf16[320,1024]{1,0:T(8,128)(2,1)S(1)} %slice.52), channel_id=1, source_target_pairs={{0,96},{32,0},{64,32},{96,64},{1,97},{33,1},{65,33},{97,65},{2,98}... | collective-permute-start | bytes 1966088 | tf_op jit(solution)/shard_map/ppermute | solution.py:18
  181.6 15.5 %collective-permute-start.26 = (bf16[512,1280]{1,0:T(8,128)(2,1)S(1)}, bf16[512,1280]{1,0:T(8,128)(2,1)S(1)}, u32[]{:S(2)}, u32[]{:S(2)}) collective-permute-start(bf16[512,1280]{1,0:T(8,128)(2,1)S(1)} %give.4), channel_id=1, source_target_pairs={{0,1},{1,0},{2,3},{3,2},{4,5},{5,4},{6,7},{7,6},{8,9},{9,8},{10,11... | collective-permute-start | bytes 3932168 | tf_op jit(solution)/shard_map/ppermute | solution.py:18
  190.4 11.2 %collective-permute-start.33 = (bf16[512,1280]{1,0:T(8,128)(2,1)S(1)}, bf16[512,1280]{1,0:T(8,128)(2,1)S(1)}, u32[]{:S(2)}, u32[]{:S(2)}) collective-permute-start(bf16[512,1280]{1,0:T(8,128)(2,1)S(1)} %give.7), channel_id=1, source_target_pairs={{0,1},{1,0},{2,3},{3,2},{4,5},{5,4},{6,7},{7,6},{8,9},{9,8},{10,11... | collective-permute-start | bytes 3932168 | tf_op jit(solution)/shard_map/ppermute | solution.py:18
  194.3 9.3 %collective-permute-start.27 = (bf16[512,1280]{1,0:T(8,128)(2,1)S(1)}, bf16[512,1280]{1,0:T(8,128)(2,1)S(1)}, u32[]{:S(2)}, u32[]{:S(2)}) collective-permute-start(bf16[512,1280]{1,0:T(8,128)(2,1)S(1)} %give.5), channel_id=1, source_target_pairs={{0,1},{1,0},{2,3},{3,2},{4,5},{5,4},{6,7},{7,6},{8,9},{9,8},{10,11... | collective-permute-start | bytes 3932168 | tf_op jit(solution)/shard_map/ppermute | solution.py:18
  196.5 11.6 %collective-permute-start.32 = (bf16[512,1280]{1,0:T(8,128)(2,1)S(1)}, bf16[512,1280]{1,0:T(8,128)(2,1)S(1)}, u32[]{:S(2)}, u32[]{:S(2)}) collective-permute-start(bf16[512,1280]{1,0:T(8,128)(2,1)S(1)} %give.6), channel_id=1, source_target_pairs={{0,1},{1,0},{2,3},{3,2},{4,5},{5,4},{6,7},{7,6},{8,9},{9,8},{10,11... | collective-permute-start | bytes 3932168 | tf_op jit(solution)/shard_map/ppermute | solution.py:18
  198.9 11.1 %collective-permute-start.34 = (bf16[128,1280]{1,0:T(8,128)(2,1)S(1)}, bf16[128,1280]{1,0:T(8,128)(2,1)S(1)}, u32[]{:S(2)}, u32[]{:S(2)}) collective-permute-start(bf16[128,1280]{1,0:T(8,128)(2,1)S(1)} %get-tuple-element.71), channel_id=1, source_target_pairs={{0,18},{1,3},{2,0},{3,17},{16,2},{17,19},{18,16},{19,1},{4,22},{5,... | collective-permute-start | bytes 983048 | tf_op jit(solution)/shard_map/ppermute | solution.py:37
  199.0 13.8 %collective-permute-start.38 = (bf16[128,1280]{1,0:T(8,128)(2,1)S(1)}, bf16[128,1280]{1,0:T(8,128)(2,1)S(1)}, u32[]{:S(2)}, u32[]{:S(2)}) collective-permute-start(bf16[128,1280]{1,0:T(8,128)(2,1)S(1)} %get-tuple-element.75), channel_id=1, source_target_pairs={{0,2},{1,19},{2,16},{3,1},{16,18},{17,3},{18,0},{19,17},{4,6},{5,2... | collective-permute-start | bytes 983048 | tf_op jit(solution)/shard_map/ppermute | solution.py:37
  203.5 12.1 %collective-permute-start.37 = (bf16[128,1280]{1,0:T(8,128)(2,1)S(1)}, bf16[128,1280]{1,0:T(8,128)(2,1)S(1)}, u32[]{:S(2)}, u32[]{:S(2)}) collective-permute-start(bf16[128,1280]{1,0:T(8,128)(2,1)S(1)} %get-tuple-element.74), channel_id=1, source_target_pairs={{0,18},{1,3},{2,0},{3,17},{16,2},{17,19},{18,16},{19,1},{4,22},{5,... | collective-permute-start | bytes 983048 | tf_op jit(solution)/shard_map/ppermute | solution.py:37
  203.6 12.7 %collective-permute-start.41 = (bf16[128,1280]{1,0:T(8,128)(2,1)S(1)}, bf16[128,1280]{1,0:T(8,128)(2,1)S(1)}, u32[]{:S(2)}, u32[]{:S(2)}) collective-permute-start(bf16[128,1280]{1,0:T(8,128)(2,1)S(1)} %get-tuple-element.78), channel_id=1, source_target_pairs={{0,2},{1,19},{2,16},{3,1},{16,18},{17,3},{18,0},{19,17},{4,6},{5,2... | collective-permute-start | bytes 983048 | tf_op jit(solution)/shard_map/ppermute | solution.py:37
  208.1 14.5 %collective-permute-start.35 = (bf16[128,1280]{1,0:T(8,128)(2,1)S(1)}, bf16[128,1280]{1,0:T(8,128)(2,1)S(1)}, u32[]{:S(2)}, u32[]{:S(2)}) collective-permute-start(bf16[128,1280]{1,0:T(8,128)(2,1)S(1)} %get-tuple-element.72), channel_id=1, source_target_pairs={{0,18},{1,3},{2,0},{3,17},{16,2},{17,19},{18,16},{19,1},{4,22},{5,... | collective-permute-start | bytes 983048 | tf_op jit(solution)/shard_map/ppermute | solution.py:37
  210.0 13.3 %collective-permute-start.39 = (bf16[128,1280]{1,0:T(8,128)(2,1)S(1)}, bf16[128,1280]{1,0:T(8,128)(2,1)S(1)}, u32[]{:S(2)}, u32[]{:S(2)}) collective-permute-start(bf16[128,1280]{1,0:T(8,128)(2,1)S(1)} %get-tuple-element.76), channel_id=1, source_target_pairs={{0,2},{1,19},{2,16},{3,1},{16,18},{17,3},{18,0},{19,17},{4,6},{5,2... | collective-permute-start | bytes 983048 | tf_op jit(solution)/shard_map/ppermute | solution.py:37
  212.7 16.9 %collective-permute-start.36 = (bf16[128,1280]{1,0:T(8,128)(2,1)S(1)}, bf16[128,1280]{1,0:T(8,128)(2,1)S(1)}, u32[]{:S(2)}, u32[]{:S(2)}) collective-permute-start(bf16[128,1280]{1,0:T(8,128)(2,1)S(1)} %get-tuple-element.73), channel_id=1, source_target_pairs={{0,18},{1,3},{2,0},{3,17},{16,2},{17,19},{18,16},{19,1},{4,22},{5,... | collective-permute-start | bytes 983048 | tf_op jit(solution)/shard_map/ppermute | solution.py:37
  215.5 14.0 %collective-permute-start.40 = (bf16[128,1280]{1,0:T(8,128)(2,1)S(1)}, bf16[128,1280]{1,0:T(8,128)(2,1)S(1)}, u32[]{:S(2)}, u32[]{:S(2)}) collective-permute-start(bf16[128,1280]{1,0:T(8,128)(2,1)S(1)} %get-tuple-element.77), channel_id=1, source_target_pairs={{0,2},{1,19},{2,16},{3,1},{16,18},{17,3},{18,0},{19,17},{4,6},{5,2... | collective-permute-start | bytes 983048 | tf_op jit(solution)/shard_map/ppermute | solution.py:37
  (13 other events, 44.9 us)
